TPU v7x, 32 devices: a whole 2x2x4 slice. The times are simulated.
32 devices in a mesh: ctx: 8 (over y, x, core), wa: 4 (over z).
Axes of the slice: x: 2, y: 2, z: 4, core: 2. Of those that a mesh axis runs over, the one named last changes fastest.
Arguments:
- block_input: bfloat16 [4, 2048, 1024], P('wa', 'ctx'), may hold values from -6 to 6
- cotangent: bfloat16 [4, 2048, 1024], P('wa', 'ctx'), may hold values from -6 to 6
- pair_order: int32 [8], replicated, may hold values from 0 to 7, each once
- norm_gains: bfloat16 [2, 1024], P(None, ('ctx', 'wa')), may hold values from 0.099609375 to 1.8984375
- norm_biases: bfloat16 [2, 1024], P(None, ('ctx', 'wa')), may hold values from -3 to 3
- w_qkv: bfloat16 [1024, 3072], P(('ctx', 'wa')), may hold values from -0.1875 to 0.1875
- attn_bias: bfloat16 [2, 1024], P(None, ('ctx', 'wa')), may hold values from -3 to 3
- w_out: bfloat16 [1024, 1024], P(('ctx', 'wa')), may hold values from -2 to 2
- resid_biases: bfloat16 [2, 1024], P(None, ('ctx', 'wa')), may hold values from -3 to 3
- w_fc: bfloat16 [1024, 4096], P(('ctx', 'wa')), may hold values from -0.1875 to 0.1875
- fc_bias: bfloat16 [4096], P(('ctx', 'wa')), may hold values from -3 to 3
- w_proj: bfloat16 [4096, 1024], P(('ctx', 'wa')), may hold values from -0.09375 to 0.09375
Outputs:
- block_output: bfloat16 [4, 2048, 1024], P('wa', 'ctx')
- input_grad: float32 [4, 2048, 1024], P('wa', 'ctx')
- norm_gains_grad: float32 [2, 1024], P(None, ('ctx', 'wa'))
- norm_biases_grad: float32 [2, 1024], P(None, ('ctx', 'wa'))
- w_qkv_grad: float32 [1024, 3072], P(('ctx', 'wa'))
- attn_bias_grad: float32 [2, 1024], P(None, ('ctx', 'wa'))
- w_out_grad: float32 [1024, 1024], P(('ctx', 'wa'))
- resid_biases_grad: float32 [2, 1024], P(None, ('ctx', 'wa'))
- w_fc_grad: float32 [1024, 4096], P(('ctx', 'wa'))
- fc_bias_grad: float32 [4096], P(('ctx', 'wa'))
- w_proj_grad: float32 [4096, 1024], P(('ctx', 'wa'))
Inputs may be any that keep to these rules, and one draw needn't show every extreme that they name: Index c of ctx holds causal blocks pair_order[c] and 15 - pair_order[c]; every value appears once.
All inputs are finite; a program needn't handle non-finite values.
Results may differ from a plain program's by a relative error of at most 0.025.
Values may be sent and summed in bfloat16 or wider, within the bound.
A program may use at most 192 MiB of HBM per device.

v0:
```python
import jax
import jax.numpy as jnp
from jax import lax
from jax.sharding import PartitionSpec as P

HEAD_DIM = 64


EPSILON = 1e-05


def normalize(field):
    average = jnp.mean(field, axis=-1, keepdims=True)
    centred = field - average
    variance = jnp.mean(centred * centred, axis=-1, keepdims=True)
    factor = lax.rsqrt(variance + EPSILON)
    return (centred * factor, factor)


def norm_back(grad_normed, normed, factor):
    return factor * (
        grad_normed
        - jnp.mean(grad_normed, axis=-1, keepdims=True)
        - normed * jnp.mean(grad_normed * normed, axis=-1, keepdims=True)
    )


def gelu_tanh(field):
    return (
        0.5
        * field
        * (1.0 + jnp.tanh(0.7978845608028654 * (field + 0.044715 * field * field * field)))
    )


def pair_positions(pair_order, block_rows):
    pair_count = pair_order.shape[0]
    blocks = jnp.stack([pair_order, 2 * pair_count - 1 - pair_order], axis=1)
    inside = jnp.arange(block_rows, dtype=jnp.int32)
    return (blocks[:, :, None] * block_rows + inside[None, None, :]).reshape(-1)


def visible(key_positions, query_positions):
    return jnp.min(key_positions) <= jnp.max(query_positions)


def block_scores(query_block, key_block, query_positions, key_positions):
    scores = (
        jnp.einsum("qhe,khe->hqk", query_block, key_block, preferred_element_type=jnp.float32)
        * 0.125
    )
    return jnp.where(key_positions[None, None, :] <= query_positions[None, :, None], scores, -1e30)


def on_device(
    block_input,
    cotangent,
    pair_order,
    norm_gains,
    norm_biases,
    w_qkv,
    attn_bias,
    w_out,
    resid_biases,
    w_fc,
    fc_bias,
    w_proj,
):
    tokens = block_input[0].astype(jnp.float32)
    row_count, model_width = tokens.shape
    half_rows = row_count // 2
    head_count = model_width // HEAD_DIM
    all_positions = pair_positions(pair_order, half_rows)
    ctx_index = lax.axis_index("ctx")
    own_positions = lax.dynamic_slice_in_dim(all_positions, ctx_index * row_count, row_count)
    full_qkv, full_out, gains, shifts, qv_bias, out_bias = (
        lax.all_gather(w_qkv, ("ctx", "wa"), axis=0, tiled=True),
        lax.all_gather(w_out, ("ctx", "wa"), axis=0, tiled=True),
        lax.all_gather(norm_gains, ("ctx", "wa"), axis=1, tiled=True),
        lax.all_gather(norm_biases, ("ctx", "wa"), axis=1, tiled=True),
        lax.all_gather(attn_bias, ("ctx", "wa"), axis=1, tiled=True),
        lax.all_gather(resid_biases, ("ctx", "wa"), axis=1, tiled=True),
    )
    gains = gains.astype(jnp.float32)
    shifts = shifts.astype(jnp.float32)
    qv_bias = qv_bias.astype(jnp.float32)
    out_bias = out_bias.astype(jnp.float32)
    first_normed, first_factor = normalize(tokens)
    first = (first_normed * gains[0] + shifts[0]).astype(jnp.bfloat16)
    projected = jnp.dot(first, full_qkv, preferred_element_type=jnp.float32)
    queries = (projected[:, :model_width] + qv_bias[0]).astype(jnp.bfloat16)
    key_rows = projected[:, model_width : 2 * model_width].astype(jnp.bfloat16)
    value_rows = (projected[:, 2 * model_width :] + qv_bias[1]).astype(jnp.bfloat16)
    all_keys, all_values = (
        lax.all_gather(key_rows, "ctx", axis=0, tiled=True),
        lax.all_gather(value_rows, "ctx", axis=0, tiled=True),
    )
    head_shape = (row_count, head_count, HEAD_DIM)
    half_shape = (half_rows, head_count, HEAD_DIM)
    query_heads = queries.reshape(head_shape)
    key_halves = all_keys.reshape((-1, 2) + half_shape)
    value_halves = all_values.reshape((-1, 2) + half_shape)
    position_halves = all_positions.reshape(-1, 2, half_rows)

    def running_half(state_pair, key_half, key_positions):
        row_max, exp_total = state_pair
        scores = block_scores(query_heads, key_half, own_positions, key_positions)
        new_max = jnp.maximum(row_max, jnp.max(scores, axis=-1))
        exp_total = exp_total * jnp.exp(row_max - new_max) + jnp.sum(
            jnp.exp(scores - new_max[:, :, None]), axis=-1
        )
        return (new_max, exp_total)

    def running(state_pair, block_item):
        keys_two, positions_two = block_item
        for half_index in range(2):
            state_pair = lax.cond(
                visible(positions_two[half_index], own_positions),
                running_half,
                lambda carried, unused_keys, unused_places: carried,
                state_pair,
                keys_two[half_index],
                positions_two[half_index],
            )
        return (state_pair, None)

    start_state = (
        jnp.full((head_count, row_count), -1e30, jnp.float32),
        jnp.zeros((head_count, row_count), jnp.float32),
    )
    (row_max, exp_total), unused = lax.scan(running, start_state, (key_halves, position_halves))
    log_total = row_max + jnp.log(exp_total)

    def weigh_half(summed, key_half, value_half, key_positions):
        scores = block_scores(query_heads, key_half, own_positions, key_positions)
        probabilities = jnp.exp(scores - log_total[:, :, None]).astype(jnp.bfloat16)
        return summed + jnp.einsum(
            "hqk,khe->qhe", probabilities, value_half, preferred_element_type=jnp.float32
        )

    def weigh(summed, block_item):
        keys_two, values_two, positions_two = block_item
        for half_index in range(2):
            summed = lax.cond(
                visible(positions_two[half_index], own_positions),
                weigh_half,
                lambda carried, unused_keys, unused_values, unused_places: carried,
                summed,
                keys_two[half_index],
                values_two[half_index],
                positions_two[half_index],
            )
        return (summed, None)

    attended, unused = lax.scan(
        weigh, jnp.zeros(head_shape, jnp.float32), (key_halves, value_halves, position_halves)
    )
    attended_low = attended.reshape(row_count, model_width).astype(jnp.bfloat16)
    branch = jnp.dot(attended_low, full_out, preferred_element_type=jnp.float32) + out_bias[0]
    hidden = tokens + branch
    full_fc, full_proj, hidden_bias = (
        lax.all_gather(w_fc, ("ctx", "wa"), axis=0, tiled=True),
        lax.all_gather(w_proj, ("ctx", "wa"), axis=0, tiled=True),
        lax.all_gather(fc_bias, ("ctx", "wa"), axis=0, tiled=True),
    )
    second_normed, second_factor = normalize(hidden)
    second = (second_normed * gains[1] + shifts[1]).astype(jnp.bfloat16)
    pre_act = jnp.dot(second, full_fc, preferred_element_type=jnp.float32) + hidden_bias.astype(
        jnp.float32
    )
    activation, gelu_pull = jax.vjp(gelu_tanh, pre_act)
    activation_low = activation.astype(jnp.bfloat16)
    output = (
        hidden
        + jnp.dot(activation_low, full_proj, preferred_element_type=jnp.float32)
        + out_bias[1]
    )
    grad_out = cotangent[0]
    grad_wide = grad_out.astype(jnp.float32)
    fc_back, proj_back = (
        lax.all_gather(w_fc, ("ctx", "wa"), axis=0, tiled=True),
        lax.all_gather(w_proj, ("ctx", "wa"), axis=0, tiled=True),
    )
    proj_grad = jnp.einsum(
        "rf,rd->fd", activation_low, grad_out, preferred_element_type=jnp.float32
    )
    proj_bias_grad = jnp.sum(grad_wide, axis=0)
    act_grad = jnp.einsum("rd,fd->rf", grad_out, proj_back, preferred_element_type=jnp.float32)
    pre_grad = gelu_pull(act_grad)[0].astype(jnp.bfloat16)
    fc_grad = jnp.einsum("rd,rf->df", second, pre_grad, preferred_element_type=jnp.float32)
    fc_bias_grad = jnp.sum(pre_grad.astype(jnp.float32), axis=0)
    second_grad = jnp.einsum("rf,df->rd", pre_grad, fc_back, preferred_element_type=jnp.float32)
    gain_two = jnp.sum(second_grad * second_normed, axis=0)
    shift_two = jnp.sum(second_grad, axis=0)
    hidden_grad = grad_wide + norm_back(second_grad * gains[1], second_normed, second_factor)
    fc_sum, proj_sum, fc_bias_sum = (
        lax.psum_scatter(fc_grad, ("ctx", "wa"), scatter_dimension=0, tiled=True),
        lax.psum_scatter(proj_grad, ("ctx", "wa"), scatter_dimension=0, tiled=True),
        lax.psum_scatter(fc_bias_grad, ("ctx", "wa"), scatter_dimension=0, tiled=True),
    )
    qkv_back, out_back = (
        lax.all_gather(w_qkv, ("ctx", "wa"), axis=0, tiled=True),
        lax.all_gather(w_out, ("ctx", "wa"), axis=0, tiled=True),
    )
    branch_grad = hidden_grad.astype(jnp.bfloat16)
    out_bias_grad = jnp.sum(branch_grad.astype(jnp.float32), axis=0)
    out_grad = jnp.einsum(
        "ra,rb->ab", attended_low, branch_grad, preferred_element_type=jnp.float32
    )
    attended_grad = jnp.einsum(
        "rb,ab->ra", branch_grad, out_back, preferred_element_type=jnp.float32
    ).astype(jnp.bfloat16)
    head_grad = attended_grad.reshape(head_shape)
    row_delta = jnp.einsum("qhe,qhe->hq", head_grad.astype(jnp.float32), attended)

    def back_half(query_grad, key_half, value_half, key_positions):
        scores = block_scores(query_heads, key_half, own_positions, key_positions)
        probabilities = jnp.exp(scores - log_total[:, :, None])
        prob_grad = jnp.einsum(
            "qhe,khe->hqk", head_grad, value_half, preferred_element_type=jnp.float32
        )
        score_grad = (probabilities * (prob_grad - row_delta[:, :, None])).astype(jnp.bfloat16)
        query_grad = (
            query_grad
            + jnp.einsum("hqk,khe->qhe", score_grad, key_half, preferred_element_type=jnp.float32)
            * 0.125
        )
        key_piece = (
            jnp.einsum("hqk,qhe->khe", score_grad, query_heads, preferred_element_type=jnp.float32)
            * 0.125
        )
        value_piece = jnp.einsum(
            "hqk,qhe->khe",
            probabilities.astype(jnp.bfloat16),
            head_grad,
            preferred_element_type=jnp.float32,
        )
        return (query_grad, key_piece, value_piece)

    def passed_half(query_grad, key_half, value_half, key_positions):
        nothing = jnp.zeros(half_shape, jnp.float32)
        return (query_grad, nothing, nothing)

    def back_pair(query_grad, block_item):
        keys_two, values_two, positions_two = block_item
        key_list = []
        value_list = []
        for half_index in range(2):
            query_grad, key_piece, value_piece = lax.cond(
                visible(positions_two[half_index], own_positions),
                back_half,
                passed_half,
                query_grad,
                keys_two[half_index],
                values_two[half_index],
                positions_two[half_index],
            )
            key_list.append(key_piece)
            value_list.append(value_piece)
        return (query_grad, (jnp.stack(key_list), jnp.stack(value_list)))

    query_grad, (key_terms, value_terms) = lax.scan(
        back_pair, jnp.zeros(head_shape, jnp.float32), (key_halves, value_halves, position_halves)
    )
    key_own, value_own = (
        lax.psum_scatter(
            key_terms.reshape(-1, model_width).astype(jnp.bfloat16),
            "ctx",
            scatter_dimension=0,
            tiled=True,
        ).astype(jnp.float32),
        lax.psum_scatter(
            value_terms.reshape(-1, model_width).astype(jnp.bfloat16),
            "ctx",
            scatter_dimension=0,
            tiled=True,
        ).astype(jnp.float32),
    )
    query_low = query_grad.reshape(row_count, model_width).astype(jnp.bfloat16)
    key_low = key_own.astype(jnp.bfloat16)
    value_low = value_own.astype(jnp.bfloat16)
    qkv_grad = jnp.concatenate([query_low, key_low, value_low], axis=1)
    qkv_weight_grad = jnp.einsum("rd,rc->dc", first, qkv_grad, preferred_element_type=jnp.float32)
    qv_bias_grad = jnp.stack(
        [
            jnp.sum(query_low.astype(jnp.float32), axis=0),
            jnp.sum(value_low.astype(jnp.float32), axis=0),
        ]
    )
    first_grad = jnp.einsum("rc,dc->rd", qkv_grad, qkv_back, preferred_element_type=jnp.float32)
    gain_one = jnp.sum(first_grad * first_normed, axis=0)
    shift_one = jnp.sum(first_grad, axis=0)
    input_grad = hidden_grad + norm_back(first_grad * gains[0], first_normed, first_factor)
    gain_grads = jnp.stack([gain_one, gain_two])
    shift_grads = jnp.stack([shift_one, shift_two])
    resid_grads = jnp.stack([out_bias_grad, proj_bias_grad])
    qkv_sum, out_sum, gain_sum, shift_sum, qv_sum, resid_sum = (
        lax.psum_scatter(qkv_weight_grad, ("ctx", "wa"), scatter_dimension=0, tiled=True),
        lax.psum_scatter(out_grad, ("ctx", "wa"), scatter_dimension=0, tiled=True),
        lax.psum_scatter(gain_grads, ("ctx", "wa"), scatter_dimension=1, tiled=True),
        lax.psum_scatter(shift_grads, ("ctx", "wa"), scatter_dimension=1, tiled=True),
        lax.psum_scatter(qv_bias_grad, ("ctx", "wa"), scatter_dimension=1, tiled=True),
        lax.psum_scatter(resid_grads, ("ctx", "wa"), scatter_dimension=1, tiled=True),
    )
    return (
        output.astype(jnp.bfloat16)[None],
        input_grad[None],
        gain_sum,
        shift_sum,
        qkv_sum,
        qv_sum,
        out_sum,
        resid_sum,
        fc_sum,
        fc_bias_sum,
        proj_sum,
    )


def solution(mesh):
    return jax.shard_map(
        on_device,
        mesh=mesh,
        in_specs=(
            P("wa", "ctx", None),
            P("wa", "ctx", None),
            P(),
            P(None, ("ctx", "wa")),
            P(None, ("ctx", "wa")),
            P(("ctx", "wa"), None),
            P(None, ("ctx", "wa")),
            P(("ctx", "wa"), None),
            P(None, ("ctx", "wa")),
            P(("ctx", "wa"), None),
            P(("ctx", "wa")),
            P(("ctx", "wa"), None),
        ),
        out_specs=(
            P("wa", "ctx", None),
            P("wa", "ctx", None),
            P(None, ("ctx", "wa")),
            P(None, ("ctx", "wa")),
            P(("ctx", "wa"), None),
            P(None, ("ctx", "wa")),
            P(("ctx", "wa"), None),
            P(None, ("ctx", "wa")),
            P(("ctx", "wa"), None),
            P(("ctx", "wa")),
            P(("ctx", "wa"), None),
        ),
        check_vma=False,
    )
```

profile of v0, /device:TPU:0, one launch (start us, length us, event | category | flops | bytes accessed | tf_op | source)
XLA Modules:
  0.0 2361.2 jit_solution(13147153251194817608)
XLA Ops:
  8.0 69.8 %all-gather.1 = bf16[32,32,2]{1,2,0:T(2,128)(2,1)S(1)} all-gather(bf16[1,32,2]{1,2,0:T(2,128)(2,1)} %bitcast.289), channel_id=1, replica_groups=mesh['ctx'=8,'wa'=4] {'ctx','wa'}, dimensions={0}, use_global_device_ids=true | all-gather | bytes 4224 | tf_op jit(solution)/shard_map/all_gather | solution.py:80
  77.8 63.2 %all-gather = bf16[32,32,2]{1,2,0:T(2,128)(2,1)S(1)} all-gather(bf16[1,32,2]{1,2,0:T(2,128)(2,1)} %bitcast.290), channel_id=1, replica_groups=mesh['ctx'=8,'wa'=4] {'ctx','wa'}, dimensions={0}, use_global_device_ids=true | all-gather | bytes 4224 | tf_op jit(solution)/shard_map/all_gather | solution.py:79
  143.7 4.9 fusion.100
  151.2 65.2 %all-gather.2 = bf16[32,32,2]{1,2,0:T(2,128)(2,1)S(1)} all-gather(bf16[1,32,2]{1,2,0:T(2,128)(2,1)S(1)} %bitcast.291), channel_id=1, replica_groups=mesh['ctx'=8,'wa'=4] {'ctx','wa'}, dimensions={0}, use_global_device_ids=true | all-gather | bytes 4224 | tf_op jit(solution)/shard_map/all_gather | solution.py:81
  221.0 63.1 %all-gather.3 = bf16[32,32,2]{1,2,0:T(2,128)(2,1)S(1)} all-gather(bf16[1,32,2]{1,2,0:T(2,128)(2,1)S(1)} %bitcast.292), channel_id=1, replica_groups=mesh['ctx'=8,'wa'=4] {'ctx','wa'}, dimensions={0}, use_global_device_ids=true | all-gather | bytes 4224 | tf_op jit(solution)/shard_map/all_gather | solution.py:82
  284.3 65.5 %all-gather.4 = bf16[32,1,128]{2,1,0:T(2,128)(2,1)S(1)} all-gather(bf16[1,1,128]{2,1,0:T(2,128)(2,1)S(1)} %bitcast.293), channel_id=1, replica_groups=mesh['ctx'=8,'wa'=4] {'ctx','wa'}, dimensions={0}, use_global_device_ids=true | all-gather | bytes 8448 | tf_op jit(solution)/shard_map/all_gather | solution.py:164
  351.4 11.8 reshape.405
  363.2 10.3 copy.72
  373.6 11.6 reshape.406
  385.2 10.4 copy.73
  395.6 60.0 %while.45 = (s32[]{:T(128)}, f32[16,256]{1,0:T(8,128)S(1)}, f32[16,256]{1,0:T(8,128)S(1)}, s32[8,2,128]{2,1,0:T(2,128)S(1)}, s32[]{:T(128)}, /*index=5*/bf16[8,2...) while((s32[]{:T(128)}, f32[16,256]{1,0:T(8,128)S(1)}, ...), condition=%wide.region_14.15_spmd, body=%wide.region_3.14_spmd.sunk | while | flops 141639936 | bytes 12164405 | solution.py:131
  455.7 57.5 %while.46 = (s32[]{:T(128)}, f32[256,16,64]{0,2,1:T(8,128)S(1)}, s32[8,2,128]{2,1,0:T(2,128)S(1)}, s32[]{:T(128)}, bf16[8,2,128,16,64]{2,4,3,1,0:T(8,128)(2,1)},...) while((s32[]{:T(128)}, f32[256,16,64]{0,2,1:T(8,128)S(1)}, ...), condition=%wide.region_22.23_spmd, body=%wide.region_15.22_spmd.sunk | while | flops 273219840 | bytes 8559897 | solution.py:155
  517.0 7.8 convolution_add_fusion
  524.8 9.3 convert_reduce_fusion
  539.6 116.2 %while.47 = (s32[]{:T(128)}, f32[256,16,64]{0,2,1:T(8,128)S(1)}, bf16[8,2,128,16,64]{2,4,3,1,0:T(8,128)(2,1)}, bf16[8,2,128,16,64]{2,4,3,1,0:T(8,128)(2,1)}, s32...) while((s32[]{:T(128)}, f32[256,16,64]{0,2,1:T(8,128)S(1)}, ...), condition=%wide.region_34.35_spmd, body=%wide.region_27.34_spmd.sunk | while | flops 682164480 | bytes 35331484 | solution.py:262
  545.2 3.4 conditional.16
  549.3 3.4 conditional.17
  560.2 3.4 conditional.16
  564.3 3.4 conditional.17
  575.1 3.4 conditional.16
  590.0 3.4 conditional.16
  594.1 3.4 conditional.17
  605.0 3.4 conditional.16
  616.6 3.4 conditional.16
  620.7 3.4 conditional.17
  631.5 3.4 conditional.16
  635.6 3.4 conditional.17
  646.4 3.4 conditional.16
  655.8 8.6 copy.79
  664.4 7.8 convert_element_type.161
  672.5 8.6 copy.78
  681.1 8.0 convert_element_type.159
  690.6 34.6 %reduce-scatter.21.cloned.1.call-done = bf16[256,1024]{0,1:T(8,128)(2,1)} async-done(((bf16[2048,1024]{0,1:T(8,128)(2,1)}), bf16[256,1024]{0,1:T(8,128)(2,1)}) %reduce-scatter.21.cloned.1.call-update) | async-done | bytes 524304 | tf_op jit(solution)/shard_map/reduce_scatter | solution.py:272
  725.2 55.1 %reduce-scatter.19.cloned.1.call-done = bf16[256,1024]{0,1:T(8,128)(2,1)} async-done(((bf16[2048,1024]{0,1:T(8,128)(2,1)}), bf16[256,1024]{0,1:T(8,128)(2,1)}) %reduce-scatter.19.cloned.1.call-update) | async-done | bytes 524304 | tf_op jit(solution)/shard_map/reduce_scatter | solution.py:266
  780.3 6.2 fusion.81
  793.8 6.5 fusion.86
  801.6 9.8 fusion.102
  812.4 10.7 fusion.88
  823.2 39.6 %all-reduce = f32[4096]{0:T(1024)S(1)} all-reduce(f32[4096]{0:T(1024)S(1)} %get-tuple-element.704), channel_id=11, replica_groups=mesh['ctx'=8,'wa'=4] {'ctx','wa'}, use_global_device_ids=true, to_apply=%region_55.56.clone | all-reduce | flops 4096 | bytes 32768
  863.4 8.2 fusion.73
  871.6 45.5 %reduce-scatter.37.cloned.1.call-done = f32[32,2]{1,0:T(8,128)} async-done(((f32[1024,2]{1,0:T(8,128)}), f32[32,2]{1,0:T(8,128)}) %reduce-scatter.37.cloned.1.call-update) | async-done | bytes 272
  921.0 128.7 %reduce-scatter.31.cloned.1.call-done = f32[32,2]{1,0:T(8,128)} async-done(((f32[1024,2]{1,0:T(8,128)}), f32[32,2]{1,0:T(8,128)}) %reduce-scatter.31.cloned.1.call-update) | async-done | bytes 272
  1051.0 131.3 %reduce-scatter.33.cloned.1.call-done = f32[32,2]{1,0:T(8,128)} async-done(((f32[1024,2]{1,0:T(8,128)}), f32[32,2]{1,0:T(8,128)}) %reduce-scatter.33.cloned.1.call-update) | async-done | bytes 272
  1183.7 131.2 %reduce-scatter.35.cloned.1.call-done = f32[32,2]{1,0:T(8,128)} async-done(((f32[1024,2]{1,0:T(8,128)}), f32[32,2]{1,0:T(8,128)}) %reduce-scatter.35.cloned.1.call-update) | async-done | bytes 272
  1316.3 146.1 %reduce-scatter.25.cloned.1.call-done = f32[32,1024]{1,0:T(8,128)} async-done(((f32[1024,1024]{1,0:T(8,128)}), f32[32,1024]{1,0:T(8,128)}) %reduce-scatter.25.cloned.1.call-update) | async-done | bytes 131088 | tf_op jit(solution)/shard_map/reduce_scatter | solution.py:299
  1462.5 160.7 %reduce-scatter.23.cloned.1.call-done = f32[32,3072]{1,0:T(8,128)} async-done(((f32[1024,3072]{1,0:T(8,128)}), f32[32,3072]{1,0:T(8,128)}) %reduce-scatter.23.cloned.1.call-update) | async-done | bytes 393232 | tf_op jit(solution)/shard_map/reduce_scatter | solution.py:298
  1623.2 366.1 %reduce-scatter.27.cloned.1.call-done = f32[32,4096]{1,0:T(8,128)} async-done(((f32[1024,4096]{1,0:T(8,128)}), f32[32,4096]{1,0:T(8,128)}) %reduce-scatter.27.cloned.1.call-update) | async-done | bytes 524304 | tf_op jit(solution)/shard_map/reduce_scatter | solution.py:197
  1989.3 365.0 %reduce-scatter.29.cloned.1.call-done = f32[128,1024]{1,0:T(8,128)} async-done(((f32[4096,1024]{1,0:T(8,128)}), f32[128,1024]{1,0:T(8,128)}) %reduce-scatter.29.cloned.1.call-update) | async-done | bytes 524304 | tf_op jit(solution)/shard_map/reduce_scatter | solution.py:198
  (504 shorter events, 254.3 us)
Async XLA Ops:
  7.2 136.5 %all-gather.12.cloned.1.call-start = ((), (), s32[]{:S(2)}) async-start(), calls=%async_computation.10 | async-start | bytes 6488064 | tf_op jit(solution)/shard_map/all_gather | solution.py:77
  7.9 343.5 %all-gather.14.cloned.1.call-start = ((), (), s32[]{:S(2)}) async-start(), calls=%async_computation.11 | async-start | bytes 4718592 | tf_op jit(solution)/shard_map/all_gather | solution.py:95
  143.7 5.0 copy-start.15
  143.7 7.5 copy-start.18
  148.6 1.7 copy-start.9
  150.3 70.7 %copy-start.19 = (bf16[2,32]{1,0:T(2,128)(2,1)S(1)}, bf16[2,32]{1,0:T(2,128)(2,1)}, u32[]{:S(2)}) copy-start(bf16[2,32]{1,0:T(2,128)(2,1)} %param.38) | copy-start | bytes 388
  150.3 133.9 %copy-start.21 = (s32[8]{0:T(128)S(1)}, s32[8]{0:T(128)}, u32[]{:S(2)}) copy-start(s32[8]{0:T(128)} %param.32) | copy-start | bytes 100
  150.3 134.0 %copy-start.20 = (bf16[128]{0:T(256)(128)(2,1)S(1)}, bf16[128]{0:T(256)(128)(2,1)}, u32[]{:S(2)}) copy-start(bf16[128]{0:T(256)(128)(2,1)} %param.40) | copy-start | bytes 772
  151.2 222.4 %all-gather.16.cloned.1.call-start = ((), (), s32[]{:S(2)}) async-start(), calls=%async_computation.12 | async-start | bytes 4718592 | tf_op jit(solution)/shard_map/all_gather | solution.py:96
  219.2 294.9 %all-gather.18.cloned.1.call-start = ((), (), s32[]{:S(2)}) async-start(), calls=%async_computation.13 | async-start | bytes 2162688 | tf_op jit(solution)/shard_map/all_gather | solution.py:78
  219.7 297.2 %all-gather.20.cloned.1.call-start = ((), (), s32[]{:S(2)}) async-start(), calls=%async_computation.14 | async-start | bytes 8650752 | tf_op jit(solution)/shard_map/all_gather | solution.py:162
  220.3 304.5 %all-gather.22.cloned.1.call-start = ((), (), s32[]{:S(2)}) async-start(), calls=%async_computation.15 | async-start | bytes 8650752 | tf_op jit(solution)/shard_map/all_gather | solution.py:163
  220.9 504.3 %reduce-scatter.21.cloned.1.call-start = ((), (), s32[]{:S(2)}) async-start(), calls=%async_computation.17 | async-start | bytes 4718592 | tf_op jit(solution)/shard_map/reduce_scatter | solution.py:272
  455.7 58.4 %copy-start.5 = (bf16[1,256,1024]{2,1,0:T(8,128)(2,1)S(1)}, bf16[1,256,1024]{2,1,0:T(8,128)(2,1)}, u32[]{:S(2)}) copy-start(bf16[1,256,1024]{2,1,0:T(8,128)(2,1)} %param.30) | copy-start | bytes 1572868
  516.6 20.3 copy-start.1
  517.0 7.9 copy-start.10
  524.8 9.3 copy-start.22
  534.2 2.7 copy-start.13
  534.2 4.2 copy-start.7
  537.4 1.0 copy-start.3
  548.6 0.7 copy-start
  563.6 0.7 copy-start
  578.5 0.7 copy-start
  593.4 0.7 copy-start
  608.4 0.7 copy-start
  620.0 0.7 copy-start
  634.9 0.7 copy-start
  649.8 0.7 copy-start
  672.2 108.0 %reduce-scatter.19.cloned.1.call-start = ((), (), s32[]{:S(2)}) async-start(), calls=%async_computation.16 | async-start | bytes 4718592 | tf_op jit(solution)/shard_map/reduce_scatter | solution.py:266
  689.1 91.1 %copy-start.6 = (bf16[1,256,1024]{2,1,0:T(8,128)(2,1)S(1)}, bf16[1,256,1024]{2,1,0:T(8,128)(2,1)}, u32[]{:S(2)}) copy-start(bf16[1,256,1024]{2,1,0:T(8,128)(2,1)} %param.30) | copy-start | bytes 1572868
  689.1 228.0 %reduce-scatter.37.cloned.1.call-start = ((), (), s32[]{:S(2)}) async-start(), calls=%async_computation.25 | async-start | bytes 540672
  690.6 359.1 %reduce-scatter.31.cloned.1.call-start = ((), (), s32[]{:S(2)}) async-start(), calls=%async_computation.22 | async-start | bytes 540672
  780.3 8.5 copy-start.12
  780.3 9.8 copy-start.8
  786.5 3.6 copy-start.4
  787.6 394.8 %reduce-scatter.33.cloned.1.call-start = ((), (), s32[]{:S(2)}) async-start(), calls=%async_computation.23 | async-start | bytes 540672
  788.7 526.3 %reduce-scatter.35.cloned.1.call-start = ((), (), s32[]{:S(2)}) async-start(), calls=%async_computation.24 | async-start | bytes 540672
  790.0 2.8 copy-start.16
  790.1 672.4 %reduce-scatter.25.cloned.1.call-start = ((), (), s32[]{:S(2)}) async-start(), calls=%async_computation.19 | async-start | bytes 4325376 | tf_op jit(solution)/shard_map/reduce_scatter | solution.py:299
  792.8 1.0 copy-start.14
  792.8 830.4 %reduce-scatter.23.cloned.1.call-start = ((), (), s32[]{:S(2)}) async-start(), calls=%async_computation.18 | async-start | bytes 12976128 | tf_op jit(solution)/shard_map/reduce_scatter | solution.py:298
  800.3 1.2 copy-start.2
  800.4 1189.0 %reduce-scatter.27.cloned.1.call-start = ((), (), s32[]{:S(2)}) async-start(), calls=%async_computation.20 | async-start | bytes 17301504 | tf_op jit(solution)/shard_map/reduce_scatter | solution.py:197
  811.4 1.0 copy-start.11
  811.4 1543.0 %reduce-scatter.29.cloned.1.call-start = ((), (), s32[]{:S(2)}) async-start(), calls=%async_computation.21 | async-start | bytes 17301504 | tf_op jit(solution)/shard_map/reduce_scatter | solution.py:198
  823.2 40.2 %copy-start.17 = (f32[1,1024]{1,0:T(1,128)S(1)}, f32[1,1024]{1,0:T(1,128)}, u32[]{:S(2)}) copy-start(f32[1,1024]{1,0:T(1,128)} %get-tuple-element.696) | copy-start | bytes 12292
Sparse Core Ops, SparseCore 0:
  10.9 72.2 all-gather.11
  151.3 34.7 all-gather.13
  219.3 32.7 all-gather.15
  254.9 56.4 all-gather.17
  314.2 76.1 all-gather.19
  393.2 75.9 all-gather.21
  672.4 52.7 reduce-scatter.20
  728.9 51.3 reduce-scatter.18
  782.5 134.5 reduce-scatter.36
  919.3 130.3 reduce-scatter.30
  1051.9 130.3 reduce-scatter.32
  1184.5 130.3 reduce-scatter.34
  1317.8 144.6 reduce-scatter.24
  1468.9 154.2 reduce-scatter.22
  1626.0 363.2 reduce-scatter.26
  1992.2 362.1 reduce-scatter.28
where the time goes:
time: 2370 us; the launch traced here: 2360 us
  waiting for transfers between devices  1570 us (66%)
  blocking collectives  366 us (15%)
  matrix products  147 us (6%)
  local copies, waits for them, and re-layouts  145 us (6%)
  loops' own time  65.6 us (3%)
  other arithmetic  53.6 us (2%)
    unnamed x20, waiting for transfers between devices  439 us
    reduce_scatter x1, waiting for transfers between devices, on_device(): lax.psum_scatter(fc_grad, ('ctx', 'wa'), scatter_dimension=0, tiled=True)  366 us
    reduce_scatter x1, waiting for transfers between devices, on_device(): lax.psum_scatter(proj_grad, ('ctx', 'wa'), scatter_dimension=0, tiled=True)  365 us
    reduce_scatter x1, waiting for transfers between devices, on_device(): lax.psum_scatter(qkv_weight_grad, ('ctx', 'wa'), scatter_dimension=0, til...  161 us
    reduce_scatter x1, waiting for transfers between devices, on_device(): lax.psum_scatter(out_grad, ('ctx', 'wa'), scatter_dimension=0, tiled=True)  146 us
    all_gather x1, blocking collectives, on_device(): lax.all_gather(norm_biases, ('ctx', 'wa'), axis=1, tiled=True)  69.8 us
    all_gather x1, blocking collectives, on_device(): lax.all_gather(fc_bias, ('ctx', 'wa'), axis=0, tiled=True)  65.5 us
    all_gather x1, blocking collectives, on_device(): lax.all_gather(attn_bias, ('ctx', 'wa'), axis=1, tiled=True)  65.2 us
  transfers between devices with their start and end apart: 16, of which 10 were waited for; matrix products, arithmetic and copies ran while one was open for 9% of the time, Pallas kernels for 0%

commit v1 on v0

v1 whole, which is shorter than its diff:
```python
import functools

import jax
import jax.numpy as jnp
from jax import lax
from jax.experimental import pallas as pl
from jax.experimental.pallas import tpu as pltpu
from jax.sharding import PartitionSpec as P

HEAD_DIM = 64
EPSILON = 1e-05
TILE = 256
BOTH = ("ctx", "wa")
LOW = jnp.bfloat16
WIDE = jnp.float32


def normalize(field):
    average = jnp.mean(field, axis=-1, keepdims=True)
    centred = field - average
    variance = jnp.mean(centred * centred, axis=-1, keepdims=True)
    factor = lax.rsqrt(variance + EPSILON)
    return (centred * factor, factor)


def norm_back(grad_normed, normed, factor):
    return factor * (
        grad_normed
        - jnp.mean(grad_normed, axis=-1, keepdims=True)
        - normed * jnp.mean(grad_normed * normed, axis=-1, keepdims=True)
    )


def gelu_tanh(field):
    return (
        0.5
        * field
        * (1.0 + jnp.tanh(0.7978845608028654 * (field + 0.044715 * field * field * field)))
    )


def contract(left, right, left_dim, right_dim):
    return lax.dot_general(
        left, right, (((left_dim,), (right_dim,)), ((), ())), preferred_element_type=WIDE
    )


def causal(shape):
    keys = lax.broadcasted_iota(jnp.int32, shape, 0)
    rows = lax.broadcasted_iota(jnp.int32, shape, 1)
    return keys <= rows


def unpack(where_ref, source_ref, targets, block, scales):
    count = source_ref.shape[0] // block
    heads = targets[0].shape[0]

    def one(index, carried):
        rows = source_ref[pl.ds(pl.multiple_of(where_ref[index] * block, block), block), :]
        place = pl.ds(pl.multiple_of(index * block, block), block)
        for part, (target, scale) in enumerate(zip(targets, scales)):
            for head in range(heads):
                start = (part * heads + head) * HEAD_DIM
                piece = rows[:, start : start + HEAD_DIM]
                if scale != 1.0:
                    piece = (piece.astype(WIDE) * scale).astype(LOW)
                target[head, place, :] = piece
        return carried

    lax.fori_loop(0, count, one, 0)


def attend_kernel(block, where_ref, qkv_ref, out_ref, log_ref, q_s, k_s, v_s):
    step = pl.program_id(0)
    heads = q_s.shape[0]

    @pl.when(step == 0)
    def _():
        unpack(where_ref, qkv_ref, (q_s, k_s, v_s), block, (0.125, 1.0, 1.0))

    here = pl.ds(pl.multiple_of(step * TILE, TILE), TILE)
    queries = [q_s[head, here, :] for head in range(heads)]

    def visit(keys_at, state, masked):
        out = []
        for head in range(heads):
            top, total, summed = state[head]
            scores = contract(k_s[head, keys_at, :], queries[head], 1, 1)
            if masked:
                scores = jnp.where(causal(scores.shape), scores, -1e30)
            new_top = jnp.maximum(top, jnp.max(scores, axis=0, keepdims=True))
            weights = jnp.exp(scores - new_top)
            shrink = jnp.exp(top - new_top)
            total = total * shrink + jnp.sum(weights, axis=0, keepdims=True)
            summed = summed * shrink + contract(
                v_s[head, keys_at, :], weights.astype(LOW), 0, 0
            )
            out.append((new_top, total, summed))
        return tuple(out)

    start = tuple(
        (
            jnp.full((1, TILE), -1e30, WIDE),
            jnp.zeros((1, TILE), WIDE),
            jnp.zeros((HEAD_DIM, TILE), WIDE),
        )
        for _ in range(heads)
    )
    state = lax.fori_loop(
        0,
        step,
        lambda j, carried: visit(pl.ds(pl.multiple_of(j * TILE, TILE), TILE), carried, False),
        start,
    )
    state = visit(here, state, True)
    pieces = []
    for head in range(heads):
        top, total, summed = state[head]
        log_ref[step, head : head + 1, :] = top + jnp.log(total)
        pieces.append((summed / total).T)
    rows = jnp.concatenate(pieces, axis=1).astype(LOW) if heads > 1 else pieces[0].astype(LOW)
    per = TILE // block
    for part in range(per):
        place = pl.multiple_of(where_ref[step * per + part] * block, block)
        out_ref[pl.ds(place, block), :] = rows[part * block : (part + 1) * block, :]


def attend(where, qkv, block):
    rows, width = qkv.shape[0], qkv.shape[1] // 3
    heads = width // HEAD_DIM
    tiles = rows // TILE
    held = pltpu.VMEM((heads, rows, HEAD_DIM), LOW)
    return pl.pallas_call(
        functools.partial(attend_kernel, block),
        grid=(tiles,),
        out_shape=(
            jax.ShapeDtypeStruct((rows, width), LOW),
            jax.ShapeDtypeStruct((tiles, heads, TILE), WIDE),
        ),
        in_specs=[
            pl.BlockSpec(memory_space=pltpu.SMEM),
            pl.BlockSpec((rows, 3 * width), lambda i: (0, 0)),
        ],
        out_specs=(
            pl.BlockSpec((rows, width), lambda i: (0, 0)),
            pl.BlockSpec((tiles, heads, TILE), lambda i: (0, 0, 0)),
        ),
        scratch_shapes=[held, held, held],
        compiler_params=pltpu.CompilerParams(vmem_limit_bytes=48 << 20),
        cost_estimate=pl.CostEstimate(
            flops=2 * rows * rows * 2 * width,
            bytes_accessed=rows * width * 8,
            transcendentals=rows * rows * heads // 2,
        ),
        name="attend",
    )(where, qkv)


def attend_back_kernel(
    block,
    where_ref,
    qkv_ref,
    attended_ref,
    grad_ref,
    log_ref,
    out_ref,
    q_s,
    k_s,
    v_s,
    a_s,
    g_s,
    dq_s,
    delta_s,
):
    step = pl.program_id(0)
    tiles = pl.num_programs(0)
    heads = q_s.shape[0]
    width = heads * HEAD_DIM

    @pl.when(step == 0)
    def _():
        unpack(where_ref, qkv_ref, (q_s, k_s, v_s), block, (0.125, 1.0, 1.0))
        unpack(where_ref, attended_ref, (a_s,), block, (1.0,))
        unpack(where_ref, grad_ref, (g_s,), block, (1.0,))
        dq_s[...] = jnp.zeros_like(dq_s)

        def one(index, carried):
            place = pl.ds(pl.multiple_of(index * TILE, TILE), TILE)
            for head in range(heads):
                product = a_s[head, place, :].astype(WIDE) * g_s[head, place, :].astype(WIDE)
                delta_s[index, head : head + 1, :] = jnp.sum(product.T, axis=0, keepdims=True)
            return carried

        lax.fori_loop(0, delta_s.shape[0], one, 0)

    here = pl.ds(pl.multiple_of(step * TILE, TILE), TILE)
    keys = [k_s[head, here, :] for head in range(heads)]
    values = [v_s[head, here, :] for head in range(heads)]

    def visit(index, state, masked):
        place = pl.ds(pl.multiple_of(index * TILE, TILE), TILE)
        out = []
        for head in range(heads):
            dk, dv = state[head]
            queries = q_s[head, place, :]
            grads = g_s[head, place, :]
            scores = contract(keys[head], queries, 1, 1)
            if masked:
                scores = jnp.where(causal(scores.shape), scores, -1e30)
            weights = jnp.exp(scores - log_ref[index, head : head + 1, :])
            pulled = contract(values[head], grads, 1, 1)
            score_grad = (weights * (pulled - delta_s[index, head : head + 1, :])).astype(LOW)
            dv = dv + contract(weights.astype(LOW), grads, 1, 0)
            dk = dk + contract(score_grad, queries, 1, 0)
            dq_s[head, place, :] += contract(score_grad, keys[head], 0, 0)
            out.append((dk, dv))
        return tuple(out)

    zero = jnp.zeros((TILE, HEAD_DIM), WIDE)
    state = visit(step, tuple((zero, zero) for _ in range(heads)), True)
    state = lax.fori_loop(step + 1, tiles, lambda i, carried: visit(i, carried, False), state)
    pieces = [dq_s[head, here, :] * 0.125 for head in range(heads)]
    pieces += [state[head][0] for head in range(heads)]
    pieces += [state[head][1] for head in range(heads)]
    rows = jnp.concatenate(pieces, axis=1).astype(LOW)
    per = TILE // block
    for part in range(per):
        place = pl.multiple_of(where_ref[step * per + part] * block, block)
        out_ref[pl.ds(place, block), :] = rows[part * block : (part + 1) * block, :]


def attend_back(where, qkv, attended, grad, logs, block):
    rows, width = attended.shape
    heads = width // HEAD_DIM
    tiles = rows // TILE
    held = pltpu.VMEM((heads, rows, HEAD_DIM), LOW)

    def whole(*shape):
        return pl.BlockSpec(shape, lambda i: (0,) * len(shape))

    return pl.pallas_call(
        functools.partial(attend_back_kernel, block),
        grid=(tiles,),
        out_shape=jax.ShapeDtypeStruct((rows, 3 * width), LOW),
        in_specs=[
            pl.BlockSpec(memory_space=pltpu.SMEM),
            whole(rows, 3 * width),
            whole(rows, width),
            whole(rows, width),
            whole(tiles, heads, TILE),
        ],
        out_specs=whole(rows, 3 * width),
        scratch_shapes=[
            held,
            held,
            held,
            held,
            held,
            pltpu.VMEM((heads, rows, HEAD_DIM), WIDE),
            pltpu.VMEM((tiles, heads, TILE), WIDE),
        ],
        compiler_params=pltpu.CompilerParams(vmem_limit_bytes=56 << 20),
        cost_estimate=pl.CostEstimate(
            flops=5 * rows * rows * 2 * width,
            bytes_accessed=rows * width * 16,
            transcendentals=rows * rows * heads // 2,
        ),
        name="attend_back",
    )(where, qkv, attended, grad, logs)


def gather_rows(rows):
    return lax.all_gather(rows, "ctx", axis=0, tiled=True)


def scatter_rows(partial):
    return lax.psum_scatter(partial, "ctx", scatter_dimension=0, tiled=True).astype(WIDE)


def on_device(
    block_input,
    cotangent,
    pair_order,
    norm_gains,
    norm_biases,
    w_qkv,
    attn_bias,
    w_out,
    resid_biases,
    w_fc,
    fc_bias,
    w_proj,
):
    ctx_count = lax.axis_size("ctx")
    wa_count = lax.axis_size("wa")
    device_count = ctx_count * wa_count
    ctx_index = lax.axis_index("ctx")
    wa_index = lax.axis_index("wa")
    tokens = block_input[0].astype(WIDE)
    row_count, model_width = tokens.shape
    block = row_count // 2
    share = model_width // device_count
    hidden_share = fc_bias.shape[0]
    width = model_width // ctx_count
    hidden_width = hidden_share * wa_count
    depth = w_qkv.shape[0]

    blocks = jnp.stack([pair_order, 2 * ctx_count - 1 - pair_order], axis=1).reshape(-1)
    numbers = jnp.arange(2 * ctx_count, dtype=jnp.int32)
    where = jnp.sum(
        jnp.where(blocks[None, :] == numbers[:, None], numbers[None, :], 0), axis=1
    ).astype(jnp.int32)

    small = jnp.concatenate(
        [
            norm_gains.reshape(-1),
            norm_biases.reshape(-1),
            attn_bias.reshape(-1),
            resid_biases.reshape(-1),
            fc_bias,
        ]
    )[None]
    small_all = lax.all_gather(small, BOTH, axis=0, tiled=True).astype(WIDE)

    def rows_of(part):
        piece = small_all[:, part * 2 * share : (part + 1) * 2 * share]
        return piece.reshape(device_count, 2, share).transpose(1, 0, 2).reshape(2, model_width)

    gains, shifts, qv_bias, out_bias = (rows_of(part) for part in range(4))
    qv_own = lax.dynamic_slice_in_dim(qv_bias, ctx_index * width, width, axis=1)
    fc_own = lax.dynamic_slice_in_dim(
        small_all[:, 8 * share :], ctx_index * wa_count, wa_count, axis=0
    ).reshape(hidden_width)

    qkv_cut = w_qkv.reshape(depth, 3, ctx_count, width).transpose(2, 0, 1, 3)
    qkv_cut = qkv_cut.reshape(ctx_count, depth, 3 * width)
    qkv_cut = lax.all_to_all(qkv_cut, "ctx", 0, 0, tiled=True)
    qkv_own = lax.all_gather(qkv_cut, "wa", axis=1, tiled=True).reshape(model_width, 3 * width)
    out_own = lax.all_gather(w_out, "wa", axis=0, tiled=True)
    fc_cut = w_fc.reshape(depth, ctx_count, hidden_width).transpose(1, 0, 2)
    fc_cut = lax.all_to_all(fc_cut, "ctx", 0, 0, tiled=True)
    fc_mat = lax.all_gather(fc_cut, "wa", axis=1, tiled=True).reshape(model_width, hidden_width)
    proj_own = lax.all_gather(w_proj, "wa", axis=0, tiled=True)

    first_normed, first_factor = normalize(tokens)
    first = gather_rows((first_normed * gains[0] + shifts[0]).astype(LOW))
    qkv_bias = jnp.concatenate([qv_own[0], jnp.zeros((width,), WIDE), qv_own[1]])
    qkv = (jnp.dot(first, qkv_own, preferred_element_type=WIDE) + qkv_bias).astype(LOW)
    attended, logs = attend(where, qkv, block)
    branch = scatter_rows(jnp.dot(attended, out_own, preferred_element_type=WIDE).astype(LOW))
    hidden = tokens + branch + out_bias[0]

    second_normed, second_factor = normalize(hidden)
    second = gather_rows((second_normed * gains[1] + shifts[1]).astype(LOW))
    pre_act = jnp.dot(second, fc_mat, preferred_element_type=WIDE) + fc_own
    activation, gelu_pull = jax.vjp(gelu_tanh, pre_act)
    activation_low = activation.astype(LOW)
    grad_out = cotangent[0]
    grad_wide = grad_out.astype(WIDE)
    grad_all = gather_rows(grad_out)
    act_grad = contract(grad_all, proj_own, 1, 1)
    pre_grad = gelu_pull(act_grad)[0].astype(LOW)
    second_grad = scatter_rows(contract(pre_grad, fc_mat, 1, 1).astype(LOW))
    output = (
        hidden
        + scatter_rows(jnp.dot(activation_low, proj_own, preferred_element_type=WIDE).astype(LOW))
        + out_bias[1]
    )

    proj_grad = contract(activation_low, grad_all, 0, 0).astype(LOW)
    proj_sum = lax.psum_scatter(proj_grad, "wa", scatter_dimension=0, tiled=True).astype(WIDE)
    fc_grad = contract(second, pre_grad, 0, 0).astype(LOW)
    fc_grad = fc_grad.reshape(ctx_count, wa_count * depth, hidden_width)
    fc_sum = lax.psum_scatter(fc_grad, "wa", scatter_dimension=1, tiled=True)
    fc_sum = lax.all_to_all(fc_sum, "ctx", 0, 0, tiled=True)
    fc_sum = fc_sum.transpose(1, 0, 2).reshape(depth, -1).astype(WIDE)
    fc_bias_grad = jnp.sum(pre_grad.astype(WIDE), axis=0)

    gain_two = jnp.sum(second_grad * second_normed, axis=0)
    shift_two = jnp.sum(second_grad, axis=0)
    hidden_grad = grad_wide + norm_back(second_grad * gains[1], second_normed, second_factor)
    branch_low = hidden_grad.astype(LOW)
    branch_grad = gather_rows(branch_low)
    attended_grad = contract(branch_grad, out_own, 1, 1).astype(LOW)
    qkv_grad = attend_back(where, qkv, attended, attended_grad, logs, block)
    first_grad = scatter_rows(contract(qkv_grad, qkv_own, 1, 1).astype(LOW))

    out_grad = contract(attended, branch_grad, 0, 0).astype(LOW)
    out_sum = lax.psum_scatter(out_grad, "wa", scatter_dimension=0, tiled=True).astype(WIDE)
    weight_grad = contract(first, qkv_grad, 0, 0).astype(LOW)
    weight_grad = weight_grad.reshape(ctx_count, wa_count * depth, 3 * width)
    qkv_sum = lax.psum_scatter(weight_grad, "wa", scatter_dimension=1, tiled=True)
    qkv_sum = lax.all_to_all(qkv_sum, "ctx", 0, 0, tiled=True)
    qkv_sum = qkv_sum.reshape(ctx_count, depth, 3, width).transpose(1, 2, 0, 3)
    qkv_sum = qkv_sum.reshape(depth, 3 * model_width).astype(WIDE)
    qkv_bias_grad = jnp.sum(qkv_grad.astype(WIDE), axis=0)

    gain_one = jnp.sum(first_grad * first_normed, axis=0)
    shift_one = jnp.sum(first_grad, axis=0)
    input_grad = hidden_grad + norm_back(first_grad * gains[0], first_normed, first_factor)

    own = (lax.broadcasted_iota(jnp.int32, (ctx_count, 1), 0) == ctx_index).astype(WIDE)

    def spread(row):
        return (own * row[None]).reshape(-1)

    pairs = [
        gain_one,
        gain_two,
        shift_one,
        shift_two,
        spread(qkv_bias_grad[:width]),
        spread(qkv_bias_grad[2 * width :]),
        jnp.sum(branch_low.astype(WIDE), axis=0),
        jnp.sum(grad_wide, axis=0),
    ]
    owned = jnp.concatenate(
        [row.reshape(device_count, share) for row in pairs]
        + [spread(fc_bias_grad).reshape(device_count, hidden_share)],
        axis=1,
    )
    summed = lax.psum(owned, BOTH)
    mine = lax.dynamic_slice_in_dim(summed, ctx_index * wa_count + wa_index, 1, axis=0)[0]
    small_grads = [
        mine[part * 2 * share : (part + 1) * 2 * share].reshape(2, share) for part in range(4)
    ]
    return (
        output.astype(LOW)[None],
        input_grad[None],
        small_grads[0],
        small_grads[1],
        qkv_sum,
        small_grads[2],
        out_sum,
        small_grads[3],
        fc_sum,
        mine[8 * share :],
        proj_sum,
    )


def solution(mesh):
    rows = P("wa", "ctx", None)
    first_dim = P(BOTH, None)
    second_dim = P(None, BOTH)
    return jax.shard_map(
        on_device,
        mesh=mesh,
        in_specs=(
            rows,
            rows,
            P(),
            second_dim,
            second_dim,
            first_dim,
            second_dim,
            first_dim,
            second_dim,
            first_dim,
            P(BOTH),
            first_dim,
        ),
        out_specs=(
            rows,
            rows,
            second_dim,
            second_dim,
            first_dim,
            second_dim,
            first_dim,
            second_dim,
            first_dim,
            P(BOTH),
            first_dim,
        ),
        check_vma=False,
    )
```

time: 2370 us -> 703 us (0.30)
  waiting for transfers between devices: 1570 us -> 337 us
  blocking collectives: 366 us -> 152 us
  local copies, waits for them, and re-layouts: 145 us -> 19.6 us
  matrix products: 147 us -> 67.3 us
  Pallas kernels: 0 us -> 69.1 us
  loops' own time: 65.6 us -> 0 us
  other arithmetic: 53.6 us -> 22 us
    reduce_scatter x6 -> x8, waiting for transfers between devices: 1130 us -> 214 us  [the longest x4 184 us: scatter_rows(): lax.psum_scatter(partial, 'ctx', scatter_dimension=0, tiled=True)]
    unnamed x20 -> x14, waiting for transfers between devices: 439 us -> 1.4 us
    all_gather x5 -> x3, blocking collectives: 327 us -> 102 us  [the longest x1 70 us: on_device(): small_all = lax.all_gather(small, BOTH, axis=0, tiled=True).astype(WIDE)]
    all_gather x6, waiting for transfers between devices: 0.07 us -> 117 us  [the longest x4 94.2 us: gather_rows(): return lax.all_gather(rows, 'ctx', axis=0, tiled=True)]
    dot_general x117 -> x12, matrix products: 147 us -> 67.3 us  [the longest x8 45.8 us: contract(): lax.dot_general(left, right, (((left_dim,), (right_dim,)), ((), ())), pre...]
    pallas_call x0 -> x2, Pallas kernels: none -> 69.1 us  [the longest x1 39.6 us: attend_back(): pl.pallas_call(functools.partial(attend_back_kernel, block), grid=(tiles,...]
    another operation x51 -> x0, loops' own time: 65.6 us -> none  [the longest x1 21.2 us: on_device(): lax.scan(back_pair, jnp.zeros(head_shape, jnp.float32), (key_halves, valu...]
    psum x0 -> x1, blocking collectives: none -> 39.8 us  [on_device(): summed = lax.psum(owned, BOTH)]
  transfers between devices with their start and end apart: 16 -> 17, of which waited for: 10 -> 11; matrix products, arithmetic and copies ran while one was open for 9% -> 9% of each run, Pallas kernels for 0% -> 6%
where the time goes in v1:
time: 703 us; the launch traced here: 696 us
  waiting for transfers between devices  337 us (48%)
  blocking collectives  152 us (22%)
  Pallas kernels  69.1 us (10%)
  matrix products  67.3 us (10%)
  other arithmetic  22 us (3%)
  local copies, waits for them, and re-layouts  19.6 us (3%)
  between operations  16.2 us (2%)
  starting transfers between devices  11.8 us (2%)
    reduce_scatter x4, waiting for transfers between devices, scatter_rows(): lax.psum_scatter(partial, 'ctx', scatter_dimension=0, tiled=True)  184 us
    all_gather x4, waiting for transfers between devices, gather_rows(): return lax.all_gather(rows, 'ctx', axis=0, tiled=True)  94.2 us
    all_gather x1, blocking collectives, on_device(): small_all = lax.all_gather(small, BOTH, axis=0, tiled=True).astype(WIDE)  70 us
    dot_general x8, matrix products, contract(): lax.dot_general(left, right, (((left_dim,), (right_dim,)), ((), ())), pre...  45.8 us
    psum x1, blocking collectives, on_device(): summed = lax.psum(owned, BOTH)  39.8 us
    pallas_call x1, Pallas kernels, attend_back(): pl.pallas_call(functools.partial(attend_back_kernel, block), grid=(tiles,...  39.6 us
    pallas_call x1, Pallas kernels, attend(): pl.pallas_call(functools.partial(attend_kernel, block), grid=(tiles,), ou...  29.5 us
    all_gather x1, waiting for transfers between devices, on_device(): proj_own = lax.all_gather(w_proj, 'wa', axis=0, tiled=True)  22.9 us
  transfers between devices with their start and end apart: 17, of which 11 were waited for; matrix products, arithmetic and copies ran while one was open for 9% of the time, Pallas kernels for 6%

profile of v1, /device:TPU:0, one launch (start us, length us, event | category | flops | bytes accessed | tf_op | source)
XLA Modules:
  0.0 695.7 jit_solution(9139232368000252397)
XLA Ops:
  11.8 1.2 convert_reduce_fusion.5
  13.0 1.3 fusion.33
  14.3 70.0 %all-gather.2 = bf16[32,1,384]{2,1,0:T(2,128)(2,1)S(1)} all-gather(bf16[1,1,384]{2,1,0:T(2,128)(2,1)S(1)} %reshape.244), channel_id=2, replica_groups=mesh['ctx'=8,'wa'=4] {'ctx','wa'}, dimensions={0}, use_global_device_ids=true | all-gather | bytes 25344 | tf_op jit(solution)/shard_map/all_gather | solution.py:323
  85.1 2.1 fusion.28
  87.3 1.0 copy.53
  89.2 3.4 all-to-all-start
  93.1 14.4 %all_gather.30 = bf16[128,1024]{1,0:T(8,128)(2,1)S(1)} all-gather(bf16[32,1024]{1,0:T(8,128)(2,1)S(1)} %copy-done.11), channel_id=1, replica_groups=mesh['ctx'=8,'wa'=4] {'wa'}, dimensions={0}, use_global_device_ids=true | all-gather | bytes 327680 | tf_op jit(solution)/shard_map/all_gather | solution.py:339
  107.7 17.5 %all_gather.29 = bf16[8,128,384]{2,1,0:T(8,128)(2,1)} all-gather(bf16[8,32,384]{2,1,0:T(8,128)(2,1)S(1)} %all-to-all-done), channel_id=1, replica_groups=mesh['ctx'=8,'wa'=4] {'wa'}, dimensions={1}, use_global_device_ids=true | all-gather | bytes 983040 | tf_op jit(solution)/shard_map/all_gather | solution.py:338
  125.1 4.7 add_convert_fusion.qkv_ref
  129.9 29.5 %attend.1 = (bf16[2048,128]{1,0:T(8,128)(2,1)S(1)}, f32[8,2,256]{2,1,0:T(2,128)S(1)}) custom-call(s32[16]{0:T(128)S(1)} %select_reduce_fusion.where_ref, bf16[2048,384]{1,0:T(8,128)(2,1)S(1)} %add_convert_fusion.qkv_ref), custom_call_target="tpu_custom_call" | custom-call | flops 2147483648 | bytes 2097152 | tf_op jit(solution)/shard_map/attend/pallas_call | solution.py:133
  160.0 3.2 convolution_convert_fusion.3
  164.3 10.7 %all_to_all.20 = bf16[8,32,512]{2,1,0:T(8,128)(2,1)S(1)} all-to-all(bf16[8,32,512]{2,1,0:T(8,128)(2,1)S(1)} %copy.46), channel_id=1, replica_groups=mesh['ctx'=8,'wa'=4] {'ctx'}, dimensions={0} | all-to-all | bytes 524288 | tf_op jit(solution)/shard_map/all_to_all | solution.py:341
  176.2 38.2 %reduce-scatter.9.cloned.1.call-done = bf16[256,1024]{1,0:T(8,128)(2,1)} async-done(((bf16[2048,1024]{1,0:T(8,128)(2,1)}), bf16[256,1024]{1,0:T(8,128)(2,1)}) %reduce-scatter.9.cloned.1.call-update) | async-done | bytes 524304 | tf_op jit(solution)/shard_map/reduce_scatter | solution.py:277
  214.4 1.3 fusion.43
  215.7 1.4 multiply_reduce_fusion
  217.1 2.2 add_convert_fusion.2
  220.8 1.5 copy.48
  222.4 33.5 %all-gather.12.cloned.1.call-done = bf16[2048,1024]{1,0:T(8,128)(2,1)} async-done(((bf16[256,1024]{1,0:T(8,128)(2,1)}), bf16[2048,1024]{1,0:T(8,128)(2,1)}) %all-gather.12.cloned.1.call-update) | async-done | bytes 4194320 | tf_op jit(solution)/shard_map/all_gather | solution.py:273
  255.9 6.5 fusion.48
  262.4 22.9 %all-gather.16.cloned.1.call-done = bf16[512,1024]{1,0:T(8,128)(2,1)} async-done(((bf16[128,1024]{1,0:T(8,128)(2,1)}), bf16[512,1024]{1,0:T(8,128)(2,1)}) %all-gather.16.cloned.1.call-update) | async-done | bytes 1048592 | tf_op jit(solution)/shard_map/all_gather | solution.py:343
  285.3 38.0 %all-gather.20.cloned.1.call-done = bf16[1,2048,1024]{2,1,0:T(8,128)(2,1)} async-done(((bf16[1,256,1024]{2,1,0:T(8,128)(2,1)}), bf16[1,2048,1024]{2,1,0:T(8,128)(2,1)}) %all-gather.20.cloned.1.call-update) | async-done | bytes 4194320 | tf_op jit(solution)/shard_map/all_gather | solution.py:273
  323.4 9.5 %convert_reduce_fusion = (f32[512]{0:T(512)S(1)}, bf16[2048,512]{1,0:T(8,128)(2,1)S(1)}) fusion(bf16[512,1024]{1,0:T(8,128)(2,1)} %all-gather.16.cloned.1.call-done, bf16[1,2048,1024]{2,1,0:T(8,128)(2,1)} %all-gather.20.cloned.1.call-done, f32[2048,512]{1,0:T(8,128)} %fusion.48, f32[512]{0:T(512)S(1)} %dynamic-slice_bitcast_fusion), kind=kOutput, calls=%fused_computation.14 | convolution fusion | flops 2175794688 | bytes 11538432 | tf_op jit(solution)/shard_map/dot_general | solution.py:43
  332.9 1.4 copy-done.15
  334.3 4.3 convolution_convert_fusion.1
  339.8 7.1 %convolution_convert_fusion.2 = bf16[2048,1024]{1,0:T(8,128)(2,1)} fusion(bf16[512,1024]{1,0:T(8,128)(2,1)S(1)} %copy-done.14, f32[2048,512]{1,0:T(8,128)} %fusion.48, f32[512]{0:T(512)S(1)} %dynamic-slice_bitcast_fusion), kind=kOutput, calls=%fused_computation.18 | convolution fusion | flops 2160066560 | bytes 9439232 | tf_op jit(solution)/shard_map/dot_general | solution.py:366
  347.0 43.1 %reduce-scatter.13.cloned.1.call-done = bf16[256,1024]{1,0:T(8,128)(2,1)} async-done(((bf16[2048,1024]{1,0:T(8,128)(2,1)}), bf16[256,1024]{1,0:T(8,128)(2,1)}) %reduce-scatter.13.cloned.1.call-update) | async-done | bytes 524304 | tf_op jit(solution)/shard_map/reduce_scatter | solution.py:277
  390.1 1.7 fusion.40
  391.8 52.9 %reduce-scatter.11.cloned.1.call-done = bf16[256,1024]{1,0:T(8,128)(2,1)} async-done(((bf16[2048,1024]{1,0:T(8,128)(2,1)}), bf16[256,1024]{1,0:T(8,128)(2,1)}) %reduce-scatter.11.cloned.1.call-update) | async-done | bytes 524304 | tf_op jit(solution)/shard_map/reduce_scatter | solution.py:277
  444.7 2.8 convert_reduce_fusion.6
  447.6 6.2 convolution_convert_fusion.5
  453.9 7.4 %fusion.12 = bf16[512,1024]{1,0:T(8,128)(2,1)} fusion(bf16[1,2048,1024]{2,1,0:T(8,128)(2,1)} %all-gather.20.cloned.1.call-done, f32[2048,512]{1,0:T(8,128)} %fusion.48, f32[512]{0:T(512)S(1)} %dynamic-slice_bitcast_fusion), kind=kOutput, calls=%fused_computation.29 | convolution fusion | flops 2158493696 | bytes 9439232 | tf_op jit(solution)/shard_map/dot_general | solution.py:43
  461.6 22.6 %all-gather.18.cloned.1.call-done = bf16[2048,1024]{1,0:T(8,128)(2,1)} async-done(((bf16[256,1024]{1,0:T(8,128)(2,1)}), bf16[2048,1024]{1,0:T(8,128)(2,1)}) %all-gather.18.cloned.1.call-update) | async-done | bytes 4194320 | tf_op jit(solution)/shard_map/all_gather | solution.py:273
  484.2 4.2 convolution_convert_fusion.4.grad_ref
  488.4 39.6 %attend_back.1 = bf16[2048,384]{1,0:T(8,128)(2,1)} custom-call(s32[16]{0:T(128)} %copy-done.2, bf16[2048,384]{1,0:T(8,128)(2,1)} %copy-done.3, bf16[2048,128]{1,0:T(8,128)(2,1)} %copy-done, bf16[2048,128]{1,0:T(8,128)(2,1)} %convolution_convert_fusion.4.grad_ref, f32[8,2,256]{2,1,0:T(2,128)} %copy-done.4), custom_call_target="tpu_custom_call" | custom-call | flops 5368709120 | bytes 4194304 | tf_op jit(solution)/shard_map/attend_back/pallas_call | solution.py:241
  528.0 4.7 convolution_convert_fusion.6
  532.9 3.7 convolution_convert_fusion.7
  536.7 5.7 convolution_convert_fusion
  542.5 3.6 all-to-all-start.3
  546.4 1.8 convert_element_type.152
  548.2 4.7 all-to-all-done.3
  554.6 11.6 %reduce-scatter.17.cloned.1.call-done = bf16[8,32,384]{2,1,0:T(8,128)(2,1)} async-done(((bf16[8,128,384]{2,1,0:T(8,128)(2,1)}), bf16[8,32,384]{2,1,0:T(8,128)(2,1)}) %reduce-scatter.17.cloned.1.call-update) | async-done | bytes 196624 | tf_op jit(solution)/shard_map/reduce_scatter | solution.py:392
  566.1 3.7 all-to-all-start.2
  569.9 18.3 %reduce-scatter.19.cloned.1.call-done = bf16[32,1024]{1,0:T(8,128)(2,1)} async-done(((bf16[128,1024]{1,0:T(8,128)(2,1)}), bf16[32,1024]{1,0:T(8,128)(2,1)}) %reduce-scatter.19.cloned.1.call-update) | async-done | bytes 65552 | tf_op jit(solution)/shard_map/reduce_scatter | solution.py:389
  588.2 1.5 convert_element_type.146
  590.9 49.9 %reduce-scatter.15.cloned.1.call-done = bf16[256,1024]{1,0:T(8,128)(2,1)} async-done(((bf16[2048,1024]{1,0:T(8,128)(2,1)}), bf16[256,1024]{1,0:T(8,128)(2,1)}) %reduce-scatter.15.cloned.1.call-update) | async-done | bytes 524304 | tf_op jit(solution)/shard_map/reduce_scatter | solution.py:277
  640.8 1.6 fusion.41
  642.7 39.8 %psum.7 = f32[32,384]{1,0:T(8,128)S(1)} all-reduce(f32[32,384]{1,0:T(8,128)S(1)} %concatenate.11), channel_id=1, replica_groups=mesh['ctx'=8,'wa'=4] {'ctx','wa'}, use_global_device_ids=true, to_apply=%region_21.22 | all-reduce | flops 12288 | bytes 98304 | tf_op jit(solution)/shard_map/psum | solution.py:422
  685.7 2.4 fusion.32
  (142 shorter events, 19.2 us)
Async XLA Ops:
  8.0 84.6 %copy-start.12 = (s32[8]{0:T(128)S(1)}, s32[8]{0:T(128)}, u32[]{:S(2)}) copy-start(s32[8]{0:T(128)} %param.14) | copy-start | bytes 100
  8.0 85.1 %copy-start.11 = (bf16[32,1024]{1,0:T(8,128)(2,1)S(1)}, bf16[32,1024]{1,0:T(8,128)(2,1)}, u32[]{:S(2)}) copy-start(bf16[32,1024]{1,0:T(8,128)(2,1)} %param.19) | copy-start | bytes 196612
  8.0 117.1 %all-gather.10.cloned.1.call-start = ((), (), s32[]{:S(2)}) async-start(), calls=%async_computation.12 | async-start | bytes 4718592 | tf_op jit(solution)/shard_map/all_gather | solution.py:273
  89.2 18.5 %all-to-all-start = ((bf16[8,32,384]{2,1,0:T(8,128)(2,1)}), bf16[8,32,384]{2,1,0:T(8,128)(2,1)S(1)}, u32[]{:S(2)}, u32[]{:S(2)}) async-start(bf16[8,32,384]{2,1,0:T(8,128)(2,1)} %reshape.218), calls=%async_computation | async-start | bytes 393216 | tf_op jit(solution)/shard_map/all_to_all | solution.py:337
  92.6 121.8 %reduce-scatter.9.cloned.1.call-start = ((), (), s32[]{:S(2)}) async-start(), calls=%async_computation.13 | async-start | bytes 4718592 | tf_op jit(solution)/shard_map/reduce_scatter | solution.py:277
  107.6 22.3 %copy-start.2 = (s32[16]{0:T(128)}, s32[16]{0:T(128)S(1)}, u32[]{:S(2)}) copy-start(s32[16]{0:T(128)S(1)} %select_reduce_fusion.where_ref) | copy-start | bytes 196
  129.9 33.3 %copy-start.3 = (bf16[2048,384]{1,0:T(8,128)(2,1)}, bf16[2048,384]{1,0:T(8,128)(2,1)S(1)}, u32[]{:S(2)}) copy-start(bf16[2048,384]{1,0:T(8,128)(2,1)S(1)} %add_convert_fusion.qkv_ref) | copy-start | bytes 4718596
  159.4 0.6 copy-start.4
  160.0 3.2 copy-start
  163.2 1.0 copy-start.10
  163.2 51.2 %copy-start.5 = (bf16[1,256,1024]{2,1,0:T(8,128)(2,1)S(1)}, bf16[1,256,1024]{2,1,0:T(8,128)(2,1)}, u32[]{:S(2)}) copy-start(bf16[1,256,1024]{2,1,0:T(8,128)(2,1)} %param.12) | copy-start | bytes 1572868
  163.2 57.6 %all-gather.14.cloned.1.call-start = ((), (), s32[]{:S(2)}) async-start(), calls=%async_computation.15 | async-start | bytes 1310720 | tf_op jit(solution)/shard_map/all_gather | solution.py:342
  175.9 80.0 %all-gather.12.cloned.1.call-start = ((), (), s32[]{:S(2)}) async-start(), calls=%async_computation.14 | async-start | bytes 4718592 | tf_op jit(solution)/shard_map/all_gather | solution.py:273
  219.2 66.1 %all-gather.16.cloned.1.call-start = ((), (), s32[]{:S(2)}) async-start(), calls=%async_computation.16 | async-start | bytes 1310720 | tf_op jit(solution)/shard_map/all_gather | solution.py:343
  219.8 103.5 %all-gather.20.cloned.1.call-start = ((), (), s32[]{:S(2)}) async-start(), calls=%async_computation.25 | async-start | bytes 4718592 | tf_op jit(solution)/shard_map/all_gather | solution.py:273
  220.6 169.5 %reduce-scatter.13.cloned.1.call-start = ((), (), s32[]{:S(2)}) async-start(), calls=%async_computation.18 | async-start | bytes 4718592 | tf_op jit(solution)/shard_map/reduce_scatter | solution.py:277
  332.9 1.4 copy-start.15
  338.6 1.2 copy-start.14
  338.6 106.1 %reduce-scatter.11.cloned.1.call-start = ((), (), s32[]{:S(2)}) async-start(), calls=%async_computation.17 | async-start | bytes 4718592 | tf_op jit(solution)/shard_map/reduce_scatter | solution.py:277
  346.9 43.2 %copy-start.6 = (bf16[256,1024]{1,0:T(8,128)(2,1)S(1)}, bf16[256,1024]{1,0:T(8,128)(2,1)}, u32[]{:S(2)}) copy-start(bf16[256,1024]{1,0:T(8,128)(2,1)} %reduce-scatter.9.cloned.1.call-done) | copy-start | bytes 1572868
  346.9 97.8 %copy-start.7 = (bf16[1,256,1024]{2,1,0:T(8,128)(2,1)S(1)}, bf16[1,256,1024]{2,1,0:T(8,128)(2,1)}, u32[]{:S(2)}) copy-start(bf16[1,256,1024]{2,1,0:T(8,128)(2,1)} %param.13) | copy-start | bytes 1572868
  346.9 137.3 %all-gather.18.cloned.1.call-start = ((), (), s32[]{:S(2)}) async-start(), calls=%async_computation.19 | async-start | bytes 4718592 | tf_op jit(solution)/shard_map/all_gather | solution.py:273
  447.5 95.0 %reduce-scatter.21.cloned.1.call-start = ((), (), s32[]{:S(2)}) async-start(), calls=%async_computation.23 | async-start | bytes 1310720 | tf_op jit(solution)/shard_map/reduce_scatter | solution.py:374
  453.8 92.6 %reduce-scatter.23.cloned.1.call-start = ((), (), s32[]{:S(2)}) async-start(), calls=%async_computation.24 | async-start | bytes 1310720 | tf_op jit(solution)/shard_map/reduce_scatter | solution.py:371
  461.3 104.9 %reduce-scatter.17.cloned.1.call-start = ((), (), s32[]{:S(2)}) async-start(), calls=%async_computation.21 | async-start | bytes 983040 | tf_op jit(solution)/shard_map/reduce_scatter | solution.py:392
  488.4 39.6 %copy-start.13 = (bf16[2048,1024]{1,0:T(8,128)(2,1)S(1)}, bf16[2048,1024]{1,0:T(8,128)(2,1)}, u32[]{:S(2)}) copy-start(bf16[2048,1024]{1,0:T(8,128)(2,1)} %all-gather.10.cloned.1.call-done) | copy-start | bytes 12582916
  528.0 4.8 copy-start.1
  532.8 3.9 copy-start.9
  532.8 55.4 %reduce-scatter.19.cloned.1.call-start = ((), (), s32[]{:S(2)}) async-start(), calls=%async_computation.22 | async-start | bytes 327680 | tf_op jit(solution)/shard_map/reduce_scatter | solution.py:389
  536.6 104.2 %reduce-scatter.15.cloned.1.call-start = ((), (), s32[]{:S(2)}) async-start(), calls=%async_computation.20 | async-start | bytes 4718592 | tf_op jit(solution)/shard_map/reduce_scatter | solution.py:277
  542.5 11.6 %copy-start.8 = (bf16[2048,384]{1,0:T(8,128)(2,1)S(1)}, bf16[2048,384]{1,0:T(8,128)(2,1)}, u32[]{:S(2)}) copy-start(bf16[2048,384]{1,0:T(8,128)(2,1)} %attend_back.1) | copy-start | bytes 4718596
  542.5 10.4 %all-to-all-start.3 = ((bf16[8,32,512]{2,1,0:T(8,128)(2,1)}), bf16[8,32,512]{2,1,0:T(8,128)(2,1)S(1)}, u32[]{:S(2)}, u32[]{:S(2)}) async-start(bf16[8,32,512]{2,1,0:T(8,128)(2,1)} %reduce-scatter.21.cloned.1.call-done), calls=%async_computation.10 | async-start | bytes 524288 | tf_op jit(solution)/shard_map/all_to_all | solution.py:375
  566.1 23.5 %all-to-all-start.2 = ((bf16[8,32,384]{2,1,0:T(8,128)(2,1)}), bf16[8,32,384]{2,1,0:T(8,128)(2,1)S(1)}, u32[]{:S(2)}, u32[]{:S(2)}) async-start(bf16[8,32,384]{2,1,0:T(8,128)(2,1)} %reduce-scatter.17.cloned.1.call-done), calls=%async_computation.7 | async-start | bytes 393216 | tf_op jit(solution)/shard_map/all_to_all | solution.py:393
Sparse Core Ops, SparseCore 0:
  87.4 32.9 all-gather.9
  163.4 50.9 reduce-scatter.8
  338.7 51.3 reduce-scatter.12
  393.3 51.3 reduce-scatter.10
Sparse Core Ops, SparseCore 1:
  176.0 25.4 all-gather.13
  219.3 36.5 all-gather.11
  257.4 27.8 all-gather.15
  287.4 35.9 all-gather.19
  447.6 36.5 all-gather.17
  487.2 27.1 reduce-scatter.20
  516.5 25.7 reduce-scatter.22
  544.6 21.5 reduce-scatter.16
  569.0 19.2 reduce-scatter.18
  591.5 49.2 reduce-scatter.14

commit v2 on v1

--- a/solution.py
+++ b/solution.py
@@ -13,6 +13,7 @@
 BOTH = ("ctx", "wa")
 LOW = jnp.bfloat16
 WIDE = jnp.float32
+MESH = pl.DeviceIdType.MESH
 
 
 def normalize(field):
@@ -273,8 +274,201 @@
     return lax.all_gather(rows, "ctx", axis=0, tiled=True)
 
 
+def greet(partners):
+    barrier = pltpu.get_barrier_semaphore()
+    for partner in partners:
+        pl.semaphore_signal(barrier, inc=1, device_id=partner, device_id_type=MESH)
+    pl.semaphore_wait(barrier, len(partners))
+
+
+def remote(source, target, send, receive, partner):
+    return pltpu.make_async_remote_copy(
+        src_ref=source,
+        dst_ref=target,
+        send_sem=send,
+        recv_sem=receive,
+        device_id=partner,
+        device_id_type=MESH,
+    )
+
+
+def scatter_kernel(
+    count,
+    partial_ref,
+    out_ref,
+    held,
+    near,
+    leaving,
+    far,
+    load_sem,
+    near_send,
+    near_recv,
+    far_send,
+    far_recv,
+):
+    chips = count // 2
+    me = lax.axis_index("ctx")
+    chip, core = me // 2, me % 2
+    sibling = {"ctx": 2 * chip + 1 - core}
+    places = [(chip + k) % chips for k in range(chips)]
+    peers = [{"ctx": 2 * place + core} for place in places]
+    loads, nears = {}, {}
+    order = list(range(1, chips)) + [0]
+    for k in order:
+        loads[k] = pltpu.make_async_copy(
+            partial_ref.at[2 * places[k] + core], held.at[k], load_sem.at[k]
+        )
+        loads[k].start()
+    greet([sibling] + peers[1:])
+    for k in order:
+        nears[k] = remote(
+            partial_ref.at[2 * places[k] + 1 - core],
+            near.at[k],
+            near_send.at[k],
+            near_recv.at[k],
+            sibling,
+        )
+        nears[k].start()
+    fars = {}
+    for k in range(1, chips):
+        loads[k].wait()
+        nears[k].wait_recv()
+        leaving[k] = (held[k].astype(WIDE) + near[k].astype(WIDE)).astype(LOW)
+        fars[k] = remote(
+            leaving.at[k], far.at[chips - k], far_send.at[k], far_recv.at[chips - k], peers[k]
+        )
+        fars[k].start()
+    loads[0].wait()
+    nears[0].wait_recv()
+    out_ref[...] = held[0].astype(WIDE) + near[0].astype(WIDE)
+    for k in range(1, chips):
+        fars[k].wait_recv()
+        out_ref[...] += far[chips - k].astype(WIDE)
+    for k in order:
+        nears[k].wait_send()
+    for k in range(1, chips):
+        fars[k].wait_send()
+
+
 def scatter_rows(partial):
-    return lax.psum_scatter(partial, "ctx", scatter_dimension=0, tiled=True).astype(WIDE)
+    count = lax.axis_size("ctx")
+    chips = count // 2
+    rows, columns = partial.shape[0] // count, partial.shape[1]
+    slots = pltpu.VMEM((chips, rows, columns), LOW)
+    sems = pltpu.SemaphoreType.DMA((chips,))
+    return pl.pallas_call(
+        functools.partial(scatter_kernel, count),
+        out_shape=jax.ShapeDtypeStruct((rows, columns), WIDE),
+        in_specs=[pl.BlockSpec(memory_space=pl.ANY)],
+        out_specs=pl.BlockSpec(memory_space=pltpu.VMEM),
+        scratch_shapes=[slots] * 4 + [sems] * 5,
+        compiler_params=pltpu.CompilerParams(
+            collective_id=2, has_side_effects=True, vmem_limit_bytes=40 << 20
+        ),
+        cost_estimate=pl.CostEstimate(
+            flops=count * rows * columns,
+            bytes_accessed=40 * count * rows * columns,
+            transcendentals=0,
+        ),
+        name="scatter_rows",
+    )(partial.reshape(count, rows, columns))
+
+
+def small_gather_kernel(ctx_count, wa_count, in_ref, out_ref, a_send, a_recv, b_send, b_recv):
+    ctx, wa = lax.axis_index("ctx"), lax.axis_index("wa")
+    along = [{"wa": (wa + k) % wa_count} for k in range(1, wa_count)]
+    across = [{"ctx": (ctx + k) % ctx_count} for k in range(1, ctx_count)]
+    greet(along + across)
+    out_ref[ctx, wa] = in_ref[...]
+    copies = [
+        remote(in_ref, out_ref.at[ctx, wa], a_send.at[k], a_recv.at[k], partner)
+        for k, partner in enumerate(along)
+    ]
+    for copy in copies:
+        copy.start()
+    for copy in copies:
+        copy.wait()
+    copies = [
+        remote(out_ref.at[ctx], out_ref.at[ctx], b_send.at[k], b_recv.at[k], partner)
+        for k, partner in enumerate(across)
+    ]
+    for copy in copies:
+        copy.start()
+    for copy in copies:
+        copy.wait()
+
+
+def small_gather(rows):
+    ctx_count, wa_count = lax.axis_size("ctx"), lax.axis_size("wa")
+    a_sems = pltpu.SemaphoreType.DMA((wa_count - 1,))
+    b_sems = pltpu.SemaphoreType.DMA((ctx_count - 1,))
+    return pl.pallas_call(
+        functools.partial(small_gather_kernel, ctx_count, wa_count),
+        out_shape=jax.ShapeDtypeStruct((ctx_count, wa_count) + rows.shape, WIDE),
+        in_specs=[pl.BlockSpec(memory_space=pltpu.VMEM)],
+        out_specs=pl.BlockSpec(memory_space=pltpu.VMEM),
+        scratch_shapes=[a_sems, a_sems, b_sems, b_sems],
+        compiler_params=pltpu.CompilerParams(collective_id=0, has_side_effects=True),
+        name="small_gather",
+    )(rows)
+
+
+def small_sum_kernel(
+    ctx_count, wa_count, in_ref, out_ref, a_s, mid_s, b_s, a_send, a_recv, b_send, b_recv
+):
+    ctx, wa = lax.axis_index("ctx"), lax.axis_index("wa")
+    greet(
+        [{"wa": (wa + k) % wa_count} for k in range(1, wa_count)]
+        + [{"ctx": (ctx + k) % ctx_count} for k in range(1, ctx_count)]
+    )
+    copies = []
+    for k in range(1, ctx_count):
+        place = (ctx + k) % ctx_count
+        copies.append(
+            remote(in_ref.at[place], a_s.at[k], a_send.at[k], a_recv.at[k], {"ctx": place})
+        )
+        copies[-1].start()
+    total = in_ref[ctx]
+    for k in range(1, ctx_count):
+        copies[k - 1].wait()
+        total = total + a_s[k]
+    mid_s[...] = total
+    copies = []
+    for k in range(1, wa_count):
+        place = (wa + k) % wa_count
+        copies.append(
+            remote(mid_s.at[place], b_s.at[k], b_send.at[k], b_recv.at[k], {"wa": place})
+        )
+        copies[-1].start()
+    total = mid_s[wa]
+    for k in range(1, wa_count):
+        copies[k - 1].wait()
+        total = total + b_s[k]
+    out_ref[...] = total
+
+
+def small_sum(parts):
+    ctx_count, wa_count = parts.shape[:2]
+    inner = parts.shape[1:]
+    a_sems = pltpu.SemaphoreType.DMA((ctx_count,))
+    b_sems = pltpu.SemaphoreType.DMA((wa_count,))
+    return pl.pallas_call(
+        functools.partial(small_sum_kernel, ctx_count, wa_count),
+        out_shape=jax.ShapeDtypeStruct(inner[1:], WIDE),
+        in_specs=[pl.BlockSpec(memory_space=pltpu.VMEM)],
+        out_specs=pl.BlockSpec(memory_space=pltpu.VMEM),
+        scratch_shapes=[
+            pltpu.VMEM(parts.shape, WIDE),
+            pltpu.VMEM(inner, WIDE),
+            pltpu.VMEM(inner, WIDE),
+            a_sems,
+            a_sems,
+            b_sems,
+            b_sems,
+        ],
+        compiler_params=pltpu.CompilerParams(collective_id=1, has_side_effects=True),
+        name="small_sum",
+    )(parts)
 
 
 def on_device(
@@ -295,7 +489,6 @@
     wa_count = lax.axis_size("wa")
     device_count = ctx_count * wa_count
     ctx_index = lax.axis_index("ctx")
-    wa_index = lax.axis_index("wa")
     tokens = block_input[0].astype(WIDE)
     row_count, model_width = tokens.shape
     block = row_count // 2
@@ -319,8 +512,11 @@
             resid_biases.reshape(-1),
             fc_bias,
         ]
-    )[None]
-    small_all = lax.all_gather(small, BOTH, axis=0, tiled=True).astype(WIDE)
+    ).astype(WIDE)
+    small_size = small.shape[0]
+    padded = -(-small_size // 1024) * 1024
+    small = jnp.pad(small, (0, padded - small_size)).reshape(-1, 128)
+    small_all = small_gather(small).reshape(device_count, padded)[:, :small_size]
 
     def rows_of(part):
         piece = small_all[:, part * 2 * share : (part + 1) * 2 * share]
@@ -419,8 +615,8 @@
         + [spread(fc_bias_grad).reshape(device_count, hidden_share)],
         axis=1,
     )
-    summed = lax.psum(owned, BOTH)
-    mine = lax.dynamic_slice_in_dim(summed, ctx_index * wa_count + wa_index, 1, axis=0)[0]
+    owned = jnp.pad(owned, ((0, 0), (0, padded - small_size)))
+    mine = small_sum(owned.reshape(ctx_count, wa_count, -1, 128)).reshape(-1)[:small_size]
     small_grads = [
         mine[part * 2 * share : (part + 1) * 2 * share].reshape(2, share) for part in range(4)
     ]

time: 703 us -> 512 us (0.73)
  waiting for transfers between devices: 337 us -> 138 us
  Pallas kernels: 69.1 us -> 210 us
  blocking collectives: 152 us -> 33.4 us
  matrix products: 67.3 us -> 57.1 us
    reduce_scatter x4 -> x0, waiting for transfers between devices: 184 us -> none  [scatter_rows(): lax.psum_scatter(partial, 'ctx', scatter_dimension=0, tiled=True)]
    pallas_call x0 -> x6, Pallas kernels: none -> 141 us  [the longest x4 116 us: scatter_rows(): pl.pallas_call(functools.partial(scatter_kernel, count), out_shape=jax.Sh...]
    all_gather x1 -> x0, blocking collectives: 70 us -> none  [on_device(): small_all = lax.all_gather(small, BOTH, axis=0, tiled=True).astype(WIDE)]
    psum x1 -> x0, blocking collectives: 39.8 us -> none  [on_device(): summed = lax.psum(owned, BOTH)]
    reduce_scatter x1, waiting for transfers between devices: 11.6 us -> 0.01 us  [on_device(): lax.psum_scatter(weight_grad, 'wa', scatter_dimension=1, tiled=True)]
    all_to_all x1 -> x0, blocking collectives: 10.7 us -> none  [on_device(): fc_cut = lax.all_to_all(fc_cut, 'ctx', 0, 0, tiled=True)]
  transfers between devices with their start and end apart: 17 -> 14, of which waited for: 11 -> 6; matrix products, arithmetic and copies ran while one was open for 9% -> 10% of each run, Pallas kernels for 6% -> 31%
where the time goes in v2:
time: 512 us; the launch traced here: 504 us
  Pallas kernels  210 us (41%)
  waiting for transfers between devices  138 us (27%)
  matrix products  57.1 us (11%)
  blocking collectives  33.4 us (7%)
  local copies, waits for them, and re-layouts  19.7 us (4%)
  other arithmetic  16.1 us (3%)
  starting transfers between devices  15.5 us (3%)
  between operations  15.2 us (3%)
    pallas_call x4, Pallas kernels, scatter_rows(): pl.pallas_call(functools.partial(scatter_kernel, count), out_shape=jax.Sh...  116 us
    all_gather x4, waiting for transfers between devices, gather_rows(): return lax.all_gather(rows, 'ctx', axis=0, tiled=True)  96.5 us
    pallas_call x1, Pallas kernels, attend_back(): pl.pallas_call(functools.partial(attend_back_kernel, block), grid=(tiles,...  39.6 us
    dot_general x8, matrix products, contract(): lax.dot_general(left, right, (((left_dim,), (right_dim,)), ((), ())), pre...  39.4 us
    pallas_call x1, Pallas kernels, attend(): pl.pallas_call(functools.partial(attend_kernel, block), grid=(tiles,), ou...  29.5 us
    all_gather x1, waiting for transfers between devices, on_device(): proj_own = lax.all_gather(w_proj, 'wa', axis=0, tiled=True)  22.9 us
    all_gather x1, blocking collectives, on_device(): lax.all_gather(qkv_cut, 'wa', axis=1, tiled=True)  19.4 us
    all_gather x1, blocking collectives, on_device(): out_own = lax.all_gather(w_out, 'wa', axis=0, tiled=True)  14 us
  transfers between devices with their start and end apart: 14, of which 6 were waited for; matrix products, arithmetic and copies ran while one was open for 10% of the time, Pallas kernels for 31%

profile of v2, /device:TPU:0, one launch (start us, length us, event | category | flops | bytes accessed | tf_op | source)
XLA Modules:
  0.0 504.4 jit_solution(13997956640841410613)
XLA Ops:
  10.3 1.2 convert_reduce_fusion.3
  11.4 1.3 fusion.31
  14.1 13.2 %small_gather.1 = f32[8,4,8,128]{3,2,1,0:T(8,128)} custom-call(f32[8,128]{1,0:T(8,128)} %bitcast_convert_fusion.in_ref), custom_call_target="tpu_custom_call" | custom-call | tf_op jit(solution)/shard_map/small_gather/pallas_call | solution.py:405
  27.4 0.9 copy.65
  29.1 2.1 fusion.24
  31.2 1.0 copy.55
  32.3 0.8 reshape.238
  33.1 3.6 all-to-all-start
  38.3 14.0 %all_gather.26 = bf16[128,1024]{1,0:T(8,128)(2,1)S(1)} all-gather(bf16[32,1024]{1,0:T(8,128)(2,1)S(1)} %copy-done.13), channel_id=1, replica_groups=mesh['ctx'=8,'wa'=4] {'wa'}, dimensions={0}, use_global_device_ids=true | all-gather | bytes 327680 | tf_op jit(solution)/shard_map/all_gather | solution.py:535
  52.4 4.0 all-to-all-start.1
  56.5 19.4 %all_gather.25 = bf16[8,128,384]{2,1,0:T(8,128)(2,1)S(1)} all-gather(bf16[8,32,384]{2,1,0:T(8,128)(2,1)S(1)} %all-to-all-done), channel_id=1, replica_groups=mesh['ctx'=8,'wa'=4] {'wa'}, dimensions={1}, use_global_device_ids=true | all-gather | bytes 983040 | tf_op jit(solution)/shard_map/all_gather | solution.py:534
  75.9 1.0 copy.49
  77.0 4.6 add_convert_fusion.qkv_ref
  81.6 29.5 %attend.1 = (bf16[2048,128]{1,0:T(8,128)(2,1)S(1)}, f32[8,2,256]{2,1,0:T(2,128)S(1)}) custom-call(s32[16]{0:T(128)S(1)} %select_reduce_fusion.where_ref, bf16[2048,384]{1,0:T(8,128)(2,1)S(1)} %add_convert_fusion.qkv_ref), custom_call_target="tpu_custom_call" | custom-call | flops 2147483648 | bytes 2097152 | tf_op jit(solution)/shard_map/attend/pallas_call | solution.py:134
  111.1 1.2 convolution_convert_fusion.3
  112.4 29.2 %scatter_rows.4 = f32[256,1024]{1,0:T(8,128)S(1)} custom-call(bf16[8,256,1024]{2,1,0:T(8,128)(2,1)S(1)} %bitcast.140), custom_call_target="tpu_custom_call" | custom-call | flops 2097152 | bytes 83886080 | tf_op jit(solution)/shard_map/scatter_rows/pallas_call | solution.py:359
  142.1 1.1 add_convert_fusion.2
  144.6 1.5 copy.50
  146.1 32.4 %all-gather.10.cloned.1.call-done = bf16[2048,1024]{1,0:T(8,128)(2,1)} async-done(((bf16[256,1024]{1,0:T(8,128)(2,1)}), bf16[2048,1024]{1,0:T(8,128)(2,1)}) %all-gather.10.cloned.1.call-update) | async-done | bytes 4194320 | tf_op jit(solution)/shard_map/all_gather | solution.py:274
  178.5 6.5 %fusion.41 = f32[2048,512]{1,0:T(8,128)} fusion(bf16[2048,1024]{1,0:T(8,128)(2,1)} %all-gather.10.cloned.1.call-done, bf16[1024,512]{1,0:T(8,128)(2,1)S(1)} %bitcast.148), kind=kOutput, calls=%fused_computation.99 | convolution fusion | flops 2147483648 | bytes 9437184 | tf_op jit(solution)/shard_map/dot_general | solution.py:551
  185.0 22.9 %all-gather.14.cloned.1.call-done = bf16[512,1024]{1,0:T(8,128)(2,1)} async-done(((bf16[128,1024]{1,0:T(8,128)(2,1)}), bf16[512,1024]{1,0:T(8,128)(2,1)}) %all-gather.14.cloned.1.call-update) | async-done | bytes 1048592 | tf_op jit(solution)/shard_map/all_gather | solution.py:539
  207.9 38.0 %all-gather.18.cloned.1.call-done = bf16[1,2048,1024]{2,1,0:T(8,128)(2,1)} async-done(((bf16[1,256,1024]{2,1,0:T(8,128)(2,1)}), bf16[1,2048,1024]{2,1,0:T(8,128)(2,1)}) %all-gather.18.cloned.1.call-update) | async-done | bytes 4194320 | tf_op jit(solution)/shard_map/all_gather | solution.py:274
  245.9 9.7 %convert_reduce_fusion = (f32[512]{0:T(512)S(1)}, bf16[2048,512]{1,0:T(8,128)(2,1)S(1)}) fusion(bf16[512,1024]{1,0:T(8,128)(2,1)} %all-gather.14.cloned.1.call-done, bf16[1,2048,1024]{2,1,0:T(8,128)(2,1)} %all-gather.18.cloned.1.call-done, f32[2048,512]{1,0:T(8,128)} %fusion.41, f32[512]{0:T(512)S(1)} %dynamic-slice_bitcast_fusion), kind=kOutput, calls=%fused_computation.14 | convolution fusion | flops 2175794688 | bytes 11538432 | tf_op jit(solution)/shard_map/dot_general | solution.py:44
  255.6 3.3 convolution_convert_fusion.5
  259.3 7.0 %fusion.12 = bf16[512,1024]{1,0:T(8,128)(2,1)} fusion(bf16[1,2048,1024]{2,1,0:T(8,128)(2,1)} %all-gather.18.cloned.1.call-done, f32[2048,512]{1,0:T(8,128)} %fusion.41, f32[512]{0:T(512)S(1)} %dynamic-slice_bitcast_fusion), kind=kOutput, calls=%fused_computation.23 | convolution fusion | flops 2158493696 | bytes 9439232 | tf_op jit(solution)/shard_map/dot_general | solution.py:44
  266.4 5.4 %convolution_convert_fusion.2 = bf16[2048,1024]{1,0:T(8,128)(2,1)S(1)} fusion(bf16[512,1024]{1,0:T(8,128)(2,1)} %all-gather.14.cloned.1.call-done, f32[2048,512]{1,0:T(8,128)} %fusion.41, f32[512]{0:T(512)S(1)} %dynamic-slice_bitcast_fusion), kind=kOutput, calls=%fused_computation.18 | convolution fusion | flops 2160066560 | bytes 9439232 | tf_op jit(solution)/shard_map/dot_general | solution.py:562
  271.8 28.9 %scatter_rows.5 = f32[256,1024]{1,0:T(8,128)S(1)} custom-call(bf16[8,256,1024]{2,1,0:T(8,128)(2,1)S(1)} %bitcast.142), custom_call_target="tpu_custom_call" | custom-call | flops 2097152 | bytes 83886080 | tf_op jit(solution)/shard_map/scatter_rows/pallas_call | solution.py:359
  300.7 2.4 convolution_convert_fusion.1
  303.1 28.8 %scatter_rows.6 = f32[256,1024]{1,0:T(8,128)S(1)} custom-call(bf16[8,256,1024]{2,1,0:T(8,128)(2,1)S(1)} %bitcast.143), custom_call_target="tpu_custom_call" | custom-call | flops 2097152 | bytes 83886080 | tf_op jit(solution)/shard_map/scatter_rows/pallas_call | solution.py:359
  332.4 1.5 convert_reduce_fusion.4
  334.1 3.4 all-to-all-start.3
  338.3 1.8 convert_element_type.137
  340.1 4.2 all-to-all-done.3
  345.3 26.0 %all-gather.16.cloned.1.call-done = bf16[2048,1024]{1,0:T(8,128)(2,1)} async-done(((bf16[256,1024]{1,0:T(8,128)(2,1)}), bf16[2048,1024]{1,0:T(8,128)(2,1)}) %all-gather.16.cloned.1.call-update) | async-done | bytes 4194320 | tf_op jit(solution)/shard_map/all_gather | solution.py:274
  371.3 4.2 convolution_convert_fusion.4.grad_ref
  375.5 39.6 %attend_back.1 = bf16[2048,384]{1,0:T(8,128)(2,1)} custom-call(s32[16]{0:T(128)} %copy-done.3, bf16[2048,384]{1,0:T(8,128)(2,1)} %copy-done.4, bf16[2048,128]{1,0:T(8,128)(2,1)} %copy-done, bf16[2048,128]{1,0:T(8,128)(2,1)} %convolution_convert_fusion.4.grad_ref, f32[8,2,256]{2,1,0:T(2,128)} %copy-done.5), custom_call_target="tpu_custom_call" | custom-call | flops 5368709120 | bytes 4194304 | tf_op jit(solution)/shard_map/attend_back/pallas_call | solution.py:242
  415.1 1.7 convert_reduce_fusion.1
  416.8 5.9 %convolution_convert_fusion = bf16[2048,1024]{1,0:T(8,128)(2,1)} fusion(bf16[2048,384]{1,0:T(8,128)(2,1)} %attend_back.1, bf16[1024,384]{1,0:T(8,128)(2,1)S(1)} %bitcast.154), kind=kOutput, calls=%fused_computation.16 | convolution fusion | flops 1612709888 | bytes 6553600 | tf_op jit(solution)/shard_map/dot_general | solution.py:44
  422.8 3.2 convolution_convert_fusion.6
  426.3 2.2 copy-done.2
  428.4 28.8 %scatter_rows.7 = f32[256,1024]{1,0:T(8,128)S(1)} custom-call(bf16[8,256,1024]{2,1,0:T(8,128)(2,1)S(1)} %bitcast.141), custom_call_target="tpu_custom_call" | custom-call | flops 2097152 | bytes 83886080 | tf_op jit(solution)/shard_map/scatter_rows/pallas_call | solution.py:359
  458.8 11.7 %small_sum.1 = f32[8,128]{1,0:T(8,128)} custom-call(f32[8,4,8,128]{3,2,1,0:T(8,128)} %bitcast.157), custom_call_target="tpu_custom_call" | custom-call | tf_op jit(solution)/shard_map/small_sum/pallas_call | solution.py:455
  471.9 3.6 convolution_convert_fusion.7
  475.6 1.3 fusion.29
  476.9 3.4 all-to-all-start.2
  480.3 1.2 slice_bitcast_fusion
  481.5 12.9 %reduce-scatter.7.cloned.1.call-done = bf16[32,1024]{1,0:T(8,128)(2,1)} async-done(((bf16[128,1024]{1,0:T(8,128)(2,1)}), bf16[32,1024]{1,0:T(8,128)(2,1)}) %reduce-scatter.7.cloned.1.call-update) | async-done | bytes 65552 | tf_op jit(solution)/shard_map/reduce_scatter | solution.py:585
  494.4 1.5 convert_element_type.131
  (141 shorter events, 16.0 us)
Async XLA Ops:
  7.2 29.6 %copy-start.14 = (s32[8]{0:T(128)S(1)}, s32[8]{0:T(128)}, u32[]{:S(2)}) copy-start(s32[8]{0:T(128)} %param.14) | copy-start | bytes 100
  7.2 30.2 %copy-start.12 = (bf16[32,4096]{1,0:T(8,128)(2,1)S(1)}, bf16[32,4096]{1,0:T(8,128)(2,1)}, u32[]{:S(2)}) copy-start(bf16[32,4096]{1,0:T(8,128)(2,1)} %param.21) | copy-start | bytes 786436
  7.2 31.1 %copy-start.13 = (bf16[32,1024]{1,0:T(8,128)(2,1)S(1)}, bf16[32,1024]{1,0:T(8,128)(2,1)}, u32[]{:S(2)}) copy-start(bf16[32,1024]{1,0:T(8,128)(2,1)} %param.19) | copy-start | bytes 196612
  7.2 69.8 %all-gather.8.cloned.1.call-start = ((), (), s32[]{:S(2)}) async-start(), calls=%async_computation.8 | async-start | bytes 4718592 | tf_op jit(solution)/shard_map/all_gather | solution.py:274
  33.1 19.3 %all-to-all-start = ((bf16[8,32,384]{2,1,0:T(8,128)(2,1)}), bf16[8,32,384]{2,1,0:T(8,128)(2,1)S(1)}, u32[]{:S(2)}, u32[]{:S(2)}) async-start(bf16[8,32,384]{2,1,0:T(8,128)(2,1)} %reshape.238), calls=%async_computation | async-start | bytes 393216 | tf_op jit(solution)/shard_map/all_to_all | solution.py:533
  52.4 29.1 %copy-start.3 = (s32[16]{0:T(128)}, s32[16]{0:T(128)S(1)}, u32[]{:S(2)}) copy-start(s32[16]{0:T(128)S(1)} %select_reduce_fusion.where_ref) | copy-start | bytes 196
  52.4 23.5 %all-to-all-start.1 = ((bf16[8,32,512]{2,1,0:T(8,128)(2,1)}), bf16[8,32,512]{2,1,0:T(8,128)(2,1)S(1)}, u32[]{:S(2)}, u32[]{:S(2)}) async-start(bf16[8,32,512]{2,1,0:T(8,128)(2,1)} %copy.48), calls=%async_computation.1 | async-start | bytes 524288 | tf_op jit(solution)/shard_map/all_to_all | solution.py:537
  56.5 88.1 %all-gather.12.cloned.1.call-start = ((), (), s32[]{:S(2)}) async-start(), calls=%async_computation.10 | async-start | bytes 1310720 | tf_op jit(solution)/shard_map/all_gather | solution.py:538
  75.9 5.6 %copy-start.10 = (bf16[8,128,384]{2,1,0:T(8,128)(2,1)}, bf16[8,128,384]{2,1,0:T(8,128)(2,1)S(1)}, u32[]{:S(2)}) copy-start(bf16[8,128,384]{2,1,0:T(8,128)(2,1)S(1)} %all_gather.25) | copy-start | bytes 2359300
  76.9 101.6 %all-gather.10.cloned.1.call-start = ((), (), s32[]{:S(2)}) async-start(), calls=%async_computation.9 | async-start | bytes 4718592 | tf_op jit(solution)/shard_map/all_gather | solution.py:274
  81.6 30.8 %copy-start.4 = (bf16[2048,384]{1,0:T(8,128)(2,1)}, bf16[2048,384]{1,0:T(8,128)(2,1)S(1)}, u32[]{:S(2)}) copy-start(bf16[2048,384]{1,0:T(8,128)(2,1)S(1)} %add_convert_fusion.qkv_ref) | copy-start | bytes 4718596
  111.0 1.3 copy-start
  111.1 1.3 copy-start.5
  112.3 29.2 %copy-start.6 = (bf16[1,256,1024]{2,1,0:T(8,128)(2,1)S(1)}, bf16[1,256,1024]{2,1,0:T(8,128)(2,1)}, u32[]{:S(2)}) copy-start(bf16[1,256,1024]{2,1,0:T(8,128)(2,1)} %param.12) | copy-start | bytes 1572868
  143.1 64.8 %all-gather.14.cloned.1.call-start = ((), (), s32[]{:S(2)}) async-start(), calls=%async_computation.11 | async-start | bytes 1310720 | tf_op jit(solution)/shard_map/all_gather | solution.py:539
  143.7 102.2 %all-gather.18.cloned.1.call-start = ((), (), s32[]{:S(2)}) async-start(), calls=%async_computation.17 | async-start | bytes 4718592 | tf_op jit(solution)/shard_map/all_gather | solution.py:274
  144.3 189.8 %reduce-scatter.9.cloned.1.call-start = ((), (), s32[]{:S(2)}) async-start(), calls=%async_computation.15 | async-start | bytes 1310720 | tf_op jit(solution)/shard_map/reduce_scatter | solution.py:570
  245.9 9.7 %copy-start.16 = (bf16[2048,1024]{1,0:T(8,128)(2,1)S(1)}, bf16[2048,1024]{1,0:T(8,128)(2,1)}, u32[]{:S(2)}) copy-start(bf16[2048,1024]{1,0:T(8,128)(2,1)} %all-gather.10.cloned.1.call-done) | copy-start | bytes 12582916
  255.6 3.4 copy-start.17
  259.0 79.4 %reduce-scatter.11.cloned.1.call-start = ((), (), s32[]{:S(2)}) async-start(), calls=%async_computation.16 | async-start | bytes 1310720 | tf_op jit(solution)/shard_map/reduce_scatter | solution.py:567
  266.3 105.0 %all-gather.16.cloned.1.call-start = ((), (), s32[]{:S(2)}) async-start(), calls=%async_computation.12 | async-start | bytes 4718592 | tf_op jit(solution)/shard_map/all_gather | solution.py:274
  271.8 28.9 %copy-start.18 = (bf16[2048,512]{1,0:T(8,128)(2,1)S(1)}, bf16[2048,512]{1,0:T(8,128)(2,1)}, u32[]{:S(2)}) copy-start(bf16[2048,512]{1,0:T(8,128)(2,1)} %copy-done.17) | copy-start | bytes 6291460
  303.0 29.4 %copy-start.8 = (bf16[1,256,1024]{2,1,0:T(8,128)(2,1)S(1)}, bf16[1,256,1024]{2,1,0:T(8,128)(2,1)}, u32[]{:S(2)}) copy-start(bf16[1,256,1024]{2,1,0:T(8,128)(2,1)} %param.13) | copy-start | bytes 1572868
  334.1 10.3 %all-to-all-start.3 = ((bf16[8,32,512]{2,1,0:T(8,128)(2,1)}), bf16[8,32,512]{2,1,0:T(8,128)(2,1)S(1)}, u32[]{:S(2)}, u32[]{:S(2)}) async-start(bf16[8,32,512]{2,1,0:T(8,128)(2,1)} %reduce-scatter.9.cloned.1.call-done), calls=%async_computation.6 | async-start | bytes 524288 | tf_op jit(solution)/shard_map/all_to_all | solution.py:571
  337.5 139.4 %reduce-scatter.5.cloned.1.call-start = ((), (), s32[]{:S(2)}) async-start(), calls=%async_computation.13 | async-start | bytes 983040 | tf_op jit(solution)/shard_map/reduce_scatter | solution.py:588
  375.5 41.3 %copy-start.11 = (bf16[8,128,384]{2,1,0:T(8,128)(2,1)S(1)}, bf16[8,128,384]{2,1,0:T(8,128)(2,1)}, u32[]{:S(2)}) copy-start(bf16[8,128,384]{2,1,0:T(8,128)(2,1)} %copy-done.10) | copy-start | bytes 2359300
  416.8 5.9 %copy-start.9 = (bf16[2048,384]{1,0:T(8,128)(2,1)S(1)}, bf16[2048,384]{1,0:T(8,128)(2,1)}, u32[]{:S(2)}) copy-start(bf16[2048,384]{1,0:T(8,128)(2,1)} %attend_back.1) | copy-start | bytes 4718596
  416.8 5.9 %copy-start.15 = (bf16[2048,1024]{1,0:T(8,128)(2,1)S(1)}, bf16[2048,1024]{1,0:T(8,128)(2,1)}, u32[]{:S(2)}) copy-start(bf16[2048,1024]{1,0:T(8,128)(2,1)} %all-gather.8.cloned.1.call-done) | copy-start | bytes 12582916
  422.8 34.5 %copy-start.7 = (bf16[1,256,1024]{2,1,0:T(8,128)(2,1)S(1)}, bf16[1,256,1024]{2,1,0:T(8,128)(2,1)}, u32[]{:S(2)}) copy-start(bf16[1,256,1024]{2,1,0:T(8,128)(2,1)} %param.12) | copy-start | bytes 1572868
  426.0 45.9 %copy-start.1 = (bf16[2048,128]{1,0:T(8,128)(2,1)S(1)}, bf16[2048,128]{1,0:T(8,128)(2,1)}, u32[]{:S(2)}) copy-start(bf16[2048,128]{1,0:T(8,128)(2,1)} %copy-done) | copy-start | bytes 1572868
  426.0 68.4 %reduce-scatter.7.cloned.1.call-start = ((), (), s32[]{:S(2)}) async-start(), calls=%async_computation.14 | async-start | bytes 327680 | tf_op jit(solution)/shard_map/reduce_scatter | solution.py:585
  426.2 2.2 copy-start.2
  476.9 19.0 %all-to-all-start.2 = ((bf16[8,32,384]{2,1,0:T(8,128)(2,1)}), bf16[8,32,384]{2,1,0:T(8,128)(2,1)S(1)}, u32[]{:S(2)}, u32[]{:S(2)}) async-start(bf16[8,32,384]{2,1,0:T(8,128)(2,1)} %reduce-scatter.5.cloned.1.call-done), calls=%async_computation.3 | async-start | bytes 393216 | tf_op jit(solution)/shard_map/all_to_all | solution.py:589
Sparse Core Ops, SparseCore 0:
  31.3 39.1 all-gather.7
  77.0 27.7 all-gather.11
  143.2 35.2 all-gather.9
  180.0 27.9 all-gather.13
  209.7 36.1 all-gather.17
  259.1 27.1 reduce-scatter.8
  288.7 25.7 reduce-scatter.10
  334.1 37.1 all-gather.15
  426.1 23.2 reduce-scatter.4
  475.7 18.6 reduce-scatter.6

commit v3 on v2

--- a/solution.py
+++ b/solution.py
@@ -543,7 +543,10 @@
     qkv_bias = jnp.concatenate([qv_own[0], jnp.zeros((width,), WIDE), qv_own[1]])
     qkv = (jnp.dot(first, qkv_own, preferred_element_type=WIDE) + qkv_bias).astype(LOW)
     attended, logs = attend(where, qkv, block)
-    branch = scatter_rows(jnp.dot(attended, out_own, preferred_element_type=WIDE).astype(LOW))
+    branch = jnp.dot(attended, out_own, preferred_element_type=WIDE).astype(LOW)
+    branch, grad_all = lax.optimization_barrier((branch, gather_rows(cotangent[0])))
+    branch = scatter_rows(branch)
+    branch, proj_own, fc_mat = lax.optimization_barrier((branch, proj_own, fc_mat))
     hidden = tokens + branch + out_bias[0]
 
     second_normed, second_factor = normalize(hidden)
@@ -553,7 +556,6 @@
     activation_low = activation.astype(LOW)
     grad_out = cotangent[0]
     grad_wide = grad_out.astype(WIDE)
-    grad_all = gather_rows(grad_out)
     act_grad = contract(grad_all, proj_own, 1, 1)
     pre_grad = gelu_pull(act_grad)[0].astype(LOW)
     second_grad = scatter_rows(contract(pre_grad, fc_mat, 1, 1).astype(LOW))

time: 512 us -> 463 us (0.904)
  waiting for transfers between devices: 138 us -> 87.4 us
  blocking collectives: 33.4 us -> 43.8 us
    all_gather x4, waiting for transfers between devices: 96.5 us -> 68.9 us  [gather_rows(): return lax.all_gather(rows, 'ctx', axis=0, tiled=True)]
    all_gather x1, waiting for transfers between devices: 22.9 us -> 0.02 us  [on_device(): proj_own = lax.all_gather(w_proj, 'wa', axis=0, tiled=True)]
    all_to_all x0 -> x1, blocking collectives: none -> 11.9 us  [on_device(): fc_cut = lax.all_to_all(fc_cut, 'ctx', 0, 0, tiled=True)]
  transfers between devices with their start and end apart: 14 -> 13, of which waited for: 6 -> 6; matrix products, arithmetic and copies ran while one was open for 10% -> 11% of each run, Pallas kernels for 31% -> 37%
where the time goes in v3:
time: 463 us; the launch traced here: 456 us
  Pallas kernels  207 us (45%)
  waiting for transfers between devices  87.4 us (19%)
  matrix products  53.4 us (12%)
  blocking collectives  43.8 us (9%)
  local copies, waits for them, and re-layouts  23 us (5%)
  between operations  15.2 us (3%)
  other arithmetic  14 us (3%)
  starting transfers between devices  11.3 us (2%)
    pallas_call x4, Pallas kernels, scatter_rows(): pl.pallas_call(functools.partial(scatter_kernel, count), out_shape=jax.Sh...  115 us
    all_gather x4, waiting for transfers between devices, gather_rows(): return lax.all_gather(rows, 'ctx', axis=0, tiled=True)  68.9 us
    pallas_call x1, Pallas kernels, attend_back(): pl.pallas_call(functools.partial(attend_back_kernel, block), grid=(tiles,...  39.6 us
    dot_general x8, matrix products, contract(): lax.dot_general(left, right, (((left_dim,), (right_dim,)), ((), ())), pre...  35.5 us
    pallas_call x1, Pallas kernels, attend(): pl.pallas_call(functools.partial(attend_kernel, block), grid=(tiles,), ou...  29.5 us
    all_gather x1, blocking collectives, on_device(): lax.all_gather(qkv_cut, 'wa', axis=1, tiled=True)  17.9 us
    all_gather x1, blocking collectives, on_device(): out_own = lax.all_gather(w_out, 'wa', axis=0, tiled=True)  13.9 us
    reduce_scatter x1, waiting for transfers between devices, on_device(): lax.psum_scatter(out_grad, 'wa', scatter_dimension=0, tiled=True)  12.8 us
  transfers between devices with their start and end apart: 13, of which 6 were waited for; matrix products, arithmetic and copies ran while one was open for 11% of the time, Pallas kernels for 37%

profile of v3, /device:TPU:0, one launch (start us, length us, event | category | flops | bytes accessed | tf_op | source)
XLA Modules:
  0.0 455.6 jit_solution(107670721834261929)
XLA Ops:
  7.3 1.1 copy.56
  8.4 11.9 %all_to_all.20 = bf16[8,32,512]{2,1,0:T(8,128)(2,1)S(1)} all-to-all(bf16[8,32,512]{2,1,0:T(8,128)(2,1)S(1)} %copy.48), channel_id=1, replica_groups=mesh['ctx'=8,'wa'=4] {'ctx'}, dimensions={0} | all-to-all | bytes 524288 | tf_op jit(solution)/shard_map/all_to_all | solution.py:537
  20.4 0.9 copy.49
  25.6 11.4 %small_gather.1 = f32[8,4,8,128]{3,2,1,0:T(8,128)} custom-call(f32[8,128]{1,0:T(8,128)} %bitcast_convert_fusion.in_ref), custom_call_target="tpu_custom_call" | custom-call | tf_op jit(solution)/shard_map/small_gather/pallas_call | solution.py:405
  37.0 0.9 copy.65
  38.8 1.2 convert_reduce_fusion.3
  40.3 1.1 fusion.15
  42.3 0.8 reshape.238
  43.1 3.4 all-to-all-start
  47.8 13.9 %all_gather.26 = bf16[128,1024]{1,0:T(8,128)(2,1)S(1)} all-gather(bf16[32,1024]{1,0:T(8,128)(2,1)S(1)} %copy-done.14), channel_id=1, replica_groups=mesh['ctx'=8,'wa'=4] {'wa'}, dimensions={0}, use_global_device_ids=true | all-gather | bytes 327680 | tf_op jit(solution)/shard_map/all_gather | solution.py:535
  61.9 17.9 %all_gather.25 = bf16[8,128,384]{2,1,0:T(8,128)(2,1)S(1)} all-gather(bf16[8,32,384]{2,1,0:T(8,128)(2,1)S(1)} %all-to-all-done), channel_id=1, replica_groups=mesh['ctx'=8,'wa'=4] {'wa'}, dimensions={1}, use_global_device_ids=true | all-gather | bytes 983040 | tf_op jit(solution)/shard_map/all_gather | solution.py:534
  79.8 2.8 copy.50
  82.6 4.9 %all-gather.8.cloned.1.call-done = bf16[2048,1024]{1,0:T(8,128)(2,1)} async-done(((bf16[256,1024]{1,0:T(8,128)(2,1)}), bf16[2048,1024]{1,0:T(8,128)(2,1)}) %all-gather.8.cloned.1.call-update) | async-done | bytes 4194320 | tf_op jit(solution)/shard_map/all_gather | solution.py:274
  87.5 4.5 add_convert_fusion.qkv_ref
  92.0 29.5 %attend.1 = (bf16[2048,128]{1,0:T(8,128)(2,1)S(1)}, f32[8,2,256]{2,1,0:T(2,128)S(1)}) custom-call(s32[16]{0:T(128)S(1)} %select_reduce_fusion.where_ref, bf16[2048,384]{1,0:T(8,128)(2,1)S(1)} %add_convert_fusion.qkv_ref), custom_call_target="tpu_custom_call" | custom-call | flops 2147483648 | bytes 2097152 | tf_op jit(solution)/shard_map/attend/pallas_call | solution.py:134
  122.1 3.2 convolution_convert_fusion.3
  126.1 2.2 copy-done
  128.3 28.8 %scatter_rows.4 = f32[256,1024]{1,0:T(8,128)S(1)} custom-call(bf16[8,256,1024]{2,1,0:T(8,128)(2,1)S(1)} %bitcast.132), custom_call_target="tpu_custom_call" | custom-call | flops 2097152 | bytes 83886080 | tf_op jit(solution)/shard_map/scatter_rows/pallas_call | solution.py:359
  157.7 1.1 add_convert_fusion.2
  159.0 37.2 %all-gather.14.cloned.1.call-done = bf16[2048,1024]{1,0:T(8,128)(2,1)} async-done(((bf16[256,1024]{1,0:T(8,128)(2,1)}), bf16[2048,1024]{1,0:T(8,128)(2,1)}) %all-gather.14.cloned.1.call-update) | async-done | bytes 4194320 | tf_op jit(solution)/shard_map/all_gather | solution.py:274
  196.2 5.0 %fusion.33 = f32[2048,512]{1,0:T(8,128)S(1)} fusion(bf16[2048,1024]{1,0:T(8,128)(2,1)} %all-gather.14.cloned.1.call-done, bf16[1024,512]{1,0:T(8,128)(2,1)} %bitcast.139), kind=kOutput, calls=%fused_computation.95 | convolution fusion | flops 2147483648 | bytes 9437184 | tf_op jit(solution)/shard_map/dot_general | solution.py:554
  201.2 5.8 %convert_reduce_fusion = (f32[512]{0:T(512)S(1)}, bf16[2048,512]{1,0:T(8,128)(2,1)S(1)}) fusion(f32[2048,512]{1,0:T(8,128)S(1)} %fusion.33, f32[512]{0:T(512)S(1)} %dynamic-slice_bitcast_fusion, bf16[2048,1024]{1,0:T(8,128)(2,1)S(1)} %bitcast.165, bf16[512,1024]{1,0:T(8,128)(2,1)S(1)} %copy-done.19), kind=kOutput, calls=%fused_computation.10 | convolution fusion | flops 2175794688 | bytes 11538432 | tf_op jit(solution)/shard_map/dot_general | solution.py:44
  207.1 3.4 convolution_convert_fusion.6
  210.7 6.9 %convolution_convert_fusion.5 = bf16[512,1024]{1,0:T(8,128)(2,1)} fusion(bf16[2048,1024]{1,0:T(8,128)(2,1)} %bitcast.164, f32[2048,512]{1,0:T(8,128)} %copy-done.22, f32[512]{0:T(512)S(1)} %dynamic-slice_bitcast_fusion), kind=kOutput, calls=%fused_computation.19 | convolution fusion | flops 2158493696 | bytes 9439232 | tf_op jit(solution)/shard_map/dot_general | solution.py:44
  217.9 5.1 %convolution_convert_fusion.2 = bf16[2048,1024]{1,0:T(8,128)(2,1)S(1)} fusion(bf16[512,1024]{1,0:T(8,128)(2,1)S(1)} %copy-done.19, f32[2048,512]{1,0:T(8,128)} %copy-done.22, f32[512]{0:T(512)S(1)} %dynamic-slice_bitcast_fusion), kind=kOutput, calls=%fused_computation.14 | convolution fusion | flops 2160066560 | bytes 9439232 | tf_op jit(solution)/shard_map/dot_general | solution.py:564
  223.0 28.9 %scatter_rows.5 = f32[256,1024]{1,0:T(8,128)S(1)} custom-call(bf16[8,256,1024]{2,1,0:T(8,128)(2,1)S(1)} %bitcast.134), custom_call_target="tpu_custom_call" | custom-call | flops 2097152 | bytes 83886080 | tf_op jit(solution)/shard_map/scatter_rows/pallas_call | solution.py:359
  251.9 2.4 convolution_convert_fusion.1
  254.3 28.8 %scatter_rows.6 = f32[256,1024]{1,0:T(8,128)S(1)} custom-call(bf16[8,256,1024]{2,1,0:T(8,128)(2,1)S(1)} %bitcast.135), custom_call_target="tpu_custom_call" | custom-call | flops 2097152 | bytes 83886080 | tf_op jit(solution)/shard_map/scatter_rows/pallas_call | solution.py:359
  283.6 1.5 convert_reduce_fusion.4
  285.3 3.4 all-to-all-start.3
  289.5 1.8 convert_element_type.137
  291.3 4.2 all-to-all-done.3
  295.6 0.8 copy.53
  296.5 26.1 %all-gather.16.cloned.1.call-done = bf16[2048,1024]{1,0:T(8,128)(2,1)} async-done(((bf16[256,1024]{1,0:T(8,128)(2,1)}), bf16[2048,1024]{1,0:T(8,128)(2,1)}) %all-gather.16.cloned.1.call-update) | async-done | bytes 4194320 | tf_op jit(solution)/shard_map/all_gather | solution.py:274
  322.5 4.2 convolution_convert_fusion.4.grad_ref
  326.8 39.6 %attend_back.1 = bf16[2048,384]{1,0:T(8,128)(2,1)} custom-call(s32[16]{0:T(128)} %copy-done.4, bf16[2048,384]{1,0:T(8,128)(2,1)} %copy-done.5, bf16[2048,128]{1,0:T(8,128)(2,1)} %copy-done.1, bf16[2048,128]{1,0:T(8,128)(2,1)} %convolution_convert_fusion.4.grad_ref, f32[8,2,256]{2,1,0:T(2,128)} %copy-done.6), custom_call_target="tpu_custom_call" | custom-call | flops 5368709120 | bytes 4194304 | tf_op jit(solution)/shard_map/attend_back/pallas_call | solution.py:242
  366.3 1.7 convert_reduce_fusion.1
  368.1 5.9 %convolution_convert_fusion = bf16[2048,1024]{1,0:T(8,128)(2,1)} fusion(bf16[2048,384]{1,0:T(8,128)(2,1)} %attend_back.1, bf16[1024,384]{1,0:T(8,128)(2,1)S(1)} %bitcast.146), kind=kOutput, calls=%fused_computation.12 | convolution fusion | flops 1612709888 | bytes 6553600 | tf_op jit(solution)/shard_map/dot_general | solution.py:44
  374.0 3.2 convolution_convert_fusion.7
  377.5 2.2 copy-done.3
  379.7 28.8 %scatter_rows.7 = f32[256,1024]{1,0:T(8,128)S(1)} custom-call(bf16[8,256,1024]{2,1,0:T(8,128)(2,1)S(1)} %bitcast.133), custom_call_target="tpu_custom_call" | custom-call | flops 2097152 | bytes 83886080 | tf_op jit(solution)/shard_map/scatter_rows/pallas_call | solution.py:359
  410.1 11.7 %small_sum.1 = f32[8,128]{1,0:T(8,128)} custom-call(f32[8,4,8,128]{3,2,1,0:T(8,128)} %bitcast.149), custom_call_target="tpu_custom_call" | custom-call | tf_op jit(solution)/shard_map/small_sum/pallas_call | solution.py:455
  423.1 3.6 convolution_convert_fusion.8
  426.8 1.3 fusion.20
  428.1 3.4 all-to-all-start.2
  431.5 1.2 slice_bitcast_fusion
  432.7 12.8 %reduce-scatter.7.cloned.1.call-done = bf16[32,1024]{1,0:T(8,128)(2,1)} async-done(((bf16[128,1024]{1,0:T(8,128)(2,1)}), bf16[32,1024]{1,0:T(8,128)(2,1)}) %reduce-scatter.7.cloned.1.call-update) | async-done | bytes 65552 | tf_op jit(solution)/shard_map/reduce_scatter | solution.py:587
  445.6 1.5 convert_element_type.131
  (148 shorter events, 16.2 us)
Async XLA Ops:
  7.2 32.8 %copy-start.7 = (bf16[1,256,1024]{2,1,0:T(8,128)(2,1)S(1)}, bf16[1,256,1024]{2,1,0:T(8,128)(2,1)}, u32[]{:S(2)}) copy-start(bf16[1,256,1024]{2,1,0:T(8,128)(2,1)} %param.12) | copy-start | bytes 1572868
  7.2 34.9 %copy-start.13 = (bf16[32,3072]{1,0:T(8,128)(2,1)S(1)}, bf16[32,3072]{1,0:T(8,128)(2,1)}, u32[]{:S(2)}) copy-start(bf16[32,3072]{1,0:T(8,128)(2,1)} %param.17) | copy-start | bytes 589828
  7.2 72.6 %all-gather.12.cloned.1.call-start = ((), (), s32[]{:S(2)}) async-start(), calls=%async_computation.10 | async-start | bytes 1310720 | tf_op jit(solution)/shard_map/all_gather | solution.py:538
  7.2 39.9 %copy-start.15 = (s32[8]{0:T(128)S(1)}, s32[8]{0:T(128)}, u32[]{:S(2)}) copy-start(s32[8]{0:T(128)} %param.14) | copy-start | bytes 100
  8.3 39.4 %copy-start.14 = (bf16[32,1024]{1,0:T(8,128)(2,1)S(1)}, bf16[32,1024]{1,0:T(8,128)(2,1)}, u32[]{:S(2)}) copy-start(bf16[32,1024]{1,0:T(8,128)(2,1)} %param.19) | copy-start | bytes 196612
  21.2 66.2 %all-gather.8.cloned.1.call-start = ((), (), s32[]{:S(2)}) async-start(), calls=%async_computation.8 | async-start | bytes 4718592 | tf_op jit(solution)/shard_map/all_gather | solution.py:274
  41.4 84.8 %all-gather.18.cloned.1.call-start = ((), (), s32[]{:S(2)}) async-start(), calls=%async_computation.17 | async-start | bytes 4718592 | tf_op jit(solution)/shard_map/all_gather | solution.py:274
  43.1 18.8 %all-to-all-start = ((bf16[8,32,384]{2,1,0:T(8,128)(2,1)}), bf16[8,32,384]{2,1,0:T(8,128)(2,1)S(1)}, u32[]{:S(2)}, u32[]{:S(2)}) async-start(bf16[8,32,384]{2,1,0:T(8,128)(2,1)} %reshape.238), calls=%async_computation | async-start | bytes 393216 | tf_op jit(solution)/shard_map/all_to_all | solution.py:533
  46.5 110.7 %all-gather.10.cloned.1.call-start = ((), (), s32[]{:S(2)}) async-start(), calls=%async_computation.9 | async-start | bytes 1310720 | tf_op jit(solution)/shard_map/all_gather | solution.py:539
  47.1 149.1 %all-gather.14.cloned.1.call-start = ((), (), s32[]{:S(2)}) async-start(), calls=%async_computation.11 | async-start | bytes 4718592 | tf_op jit(solution)/shard_map/all_gather | solution.py:274
  61.8 30.2 %copy-start.4 = (s32[16]{0:T(128)}, s32[16]{0:T(128)S(1)}, u32[]{:S(2)}) copy-start(s32[16]{0:T(128)S(1)} %select_reduce_fusion.where_ref) | copy-start | bytes 196
  79.8 7.7 %copy-start.11 = (bf16[8,128,384]{2,1,0:T(8,128)(2,1)}, bf16[8,128,384]{2,1,0:T(8,128)(2,1)S(1)}, u32[]{:S(2)}) copy-start(bf16[8,128,384]{2,1,0:T(8,128)(2,1)S(1)} %all_gather.25) | copy-start | bytes 2359300
  92.0 33.3 %copy-start.5 = (bf16[2048,384]{1,0:T(8,128)(2,1)}, bf16[2048,384]{1,0:T(8,128)(2,1)S(1)}, u32[]{:S(2)}) copy-start(bf16[2048,384]{1,0:T(8,128)(2,1)S(1)} %add_convert_fusion.qkv_ref) | copy-start | bytes 4718596
  121.5 0.6 copy-start.6
  122.1 3.2 copy-start.1
  126.1 2.2 copy-start
  158.7 126.5 %reduce-scatter.9.cloned.1.call-start = ((), (), s32[]{:S(2)}) async-start(), calls=%async_computation.15 | async-start | bytes 1310720 | tf_op jit(solution)/shard_map/reduce_scatter | solution.py:572
  159.0 42.2 %copy-start.19 = (bf16[512,1024]{1,0:T(8,128)(2,1)S(1)}, bf16[512,1024]{1,0:T(8,128)(2,1)}, u32[]{:S(2)}) copy-start(bf16[512,1024]{1,0:T(8,128)(2,1)} %all-gather.10.cloned.1.call-done) | copy-start | bytes 3145732
  196.2 5.0 %copy-start.17 = (bf16[1,2048,1024]{2,1,0:T(8,128)(2,1)S(1)}, bf16[1,2048,1024]{2,1,0:T(8,128)(2,1)}, u32[]{:S(2)}) copy-start(bf16[1,2048,1024]{2,1,0:T(8,128)(2,1)} %all-gather.18.cloned.1.call-done) | copy-start | bytes 12582916
  201.2 5.8 %copy-start.22 = (f32[2048,512]{1,0:T(8,128)}, f32[2048,512]{1,0:T(8,128)S(1)}, u32[]{:S(2)}) copy-start(f32[2048,512]{1,0:T(8,128)S(1)} %fusion.33) | copy-start | bytes 12582916
  201.2 5.8 %copy-start.18 = (bf16[2048,1024]{1,0:T(8,128)(2,1)S(1)}, bf16[2048,1024]{1,0:T(8,128)(2,1)}, u32[]{:S(2)}) copy-start(bf16[2048,1024]{1,0:T(8,128)(2,1)} %all-gather.14.cloned.1.call-done) | copy-start | bytes 12582916
  207.1 3.4 copy-start.20
  210.5 79.0 %reduce-scatter.11.cloned.1.call-start = ((), (), s32[]{:S(2)}) async-start(), calls=%async_computation.16 | async-start | bytes 1310720 | tf_op jit(solution)/shard_map/reduce_scatter | solution.py:569
  217.6 104.9 %all-gather.16.cloned.1.call-start = ((), (), s32[]{:S(2)}) async-start(), calls=%async_computation.12 | async-start | bytes 4718592 | tf_op jit(solution)/shard_map/all_gather | solution.py:274
  222.9 28.9 %copy-start.10 = (bf16[8,128,512]{2,1,0:T(8,128)(2,1)S(1)}, bf16[8,128,512]{2,1,0:T(8,128)(2,1)}, u32[]{:S(2)}) copy-start(bf16[8,128,512]{2,1,0:T(8,128)(2,1)} %copy.50) | copy-start | bytes 3145732
  223.0 28.9 %copy-start.21 = (bf16[2048,512]{1,0:T(8,128)(2,1)S(1)}, bf16[2048,512]{1,0:T(8,128)(2,1)}, u32[]{:S(2)}) copy-start(bf16[2048,512]{1,0:T(8,128)(2,1)} %copy-done.20) | copy-start | bytes 6291460
  254.2 29.4 %copy-start.8 = (bf16[1,256,1024]{2,1,0:T(8,128)(2,1)S(1)}, bf16[1,256,1024]{2,1,0:T(8,128)(2,1)}, u32[]{:S(2)}) copy-start(bf16[1,256,1024]{2,1,0:T(8,128)(2,1)} %param.13) | copy-start | bytes 1572868
  285.3 10.3 %all-to-all-start.3 = ((bf16[8,32,512]{2,1,0:T(8,128)(2,1)}), bf16[8,32,512]{2,1,0:T(8,128)(2,1)S(1)}, u32[]{:S(2)}, u32[]{:S(2)}) async-start(bf16[8,32,512]{2,1,0:T(8,128)(2,1)} %reduce-scatter.9.cloned.1.call-done), calls=%async_computation.6 | async-start | bytes 524288 | tf_op jit(solution)/shard_map/all_to_all | solution.py:573
  288.7 139.4 %reduce-scatter.5.cloned.1.call-start = ((), (), s32[]{:S(2)}) async-start(), calls=%async_computation.13 | async-start | bytes 983040 | tf_op jit(solution)/shard_map/reduce_scatter | solution.py:590
  326.8 41.3 %copy-start.12 = (bf16[8,128,384]{2,1,0:T(8,128)(2,1)S(1)}, bf16[8,128,384]{2,1,0:T(8,128)(2,1)}, u32[]{:S(2)}) copy-start(bf16[8,128,384]{2,1,0:T(8,128)(2,1)} %copy-done.11) | copy-start | bytes 2359300
  368.0 5.9 %copy-start.9 = (bf16[2048,384]{1,0:T(8,128)(2,1)S(1)}, bf16[2048,384]{1,0:T(8,128)(2,1)}, u32[]{:S(2)}) copy-start(bf16[2048,384]{1,0:T(8,128)(2,1)} %attend_back.1) | copy-start | bytes 4718596
  368.1 5.9 %copy-start.16 = (bf16[2048,1024]{1,0:T(8,128)(2,1)S(1)}, bf16[2048,1024]{1,0:T(8,128)(2,1)}, u32[]{:S(2)}) copy-start(bf16[2048,1024]{1,0:T(8,128)(2,1)} %all-gather.8.cloned.1.call-done) | copy-start | bytes 12582916
  377.2 45.9 %copy-start.2 = (bf16[2048,128]{1,0:T(8,128)(2,1)S(1)}, bf16[2048,128]{1,0:T(8,128)(2,1)}, u32[]{:S(2)}) copy-start(bf16[2048,128]{1,0:T(8,128)(2,1)} %copy-done.1) | copy-start | bytes 1572868
  377.2 68.3 %reduce-scatter.7.cloned.1.call-start = ((), (), s32[]{:S(2)}) async-start(), calls=%async_computation.14 | async-start | bytes 327680 | tf_op jit(solution)/shard_map/reduce_scatter | solution.py:587
  377.5 2.2 copy-start.3
  428.1 19.0 %all-to-all-start.2 = ((bf16[8,32,384]{2,1,0:T(8,128)(2,1)}), bf16[8,32,384]{2,1,0:T(8,128)(2,1)S(1)}, u32[]{:S(2)}, u32[]{:S(2)}) async-start(bf16[8,32,384]{2,1,0:T(8,128)(2,1)} %reduce-scatter.5.cloned.1.call-done), calls=%async_computation.3 | async-start | bytes 393216 | tf_op jit(solution)/shard_map/all_to_all | solution.py:591
Sparse Core Ops, SparseCore 0:
  21.3 27.8 all-gather.11
  51.7 35.7 all-gather.7
  89.3 36.7 all-gather.17
  127.6 28.0 all-gather.9
  158.9 37.3 all-gather.13
  210.7 27.1 reduce-scatter.8
  240.2 25.7 reduce-scatter.10
  285.3 37.2 all-gather.15
  377.4 23.2 reduce-scatter.4
  426.9 18.6 reduce-scatter.6
